TPU v7x, 32 devices: a whole 2x2x4 slice. The times are simulated.
32 devices in a mesh: dp: 4 (over y, core), context: 8 (over z, x).
Axes of the slice: x: 2, y: 2, z: 4, core: 2. Of those that a mesh axis runs over, the one named last changes fastest.
Arguments:
- query_in: bfloat16 [4, 1024, 8192], P('dp', 'context'), may hold values from -6 to 6
- key_in: bfloat16 [4, 1024, 8192], P('dp', 'context'), may hold values from -6 to 6
- value_in: bfloat16 [4, 1024, 8192], P('dp', 'context'), may hold values from -6 to 6
- grad_out: bfloat16 [4, 1024, 8192], P('dp', 'context'), may hold values from -6 to 6
- med_filter: float32 [8192, 128], P('context', 'dp'), may hold values from -0.5 to 0.5
- short_filter: float32 [3, 8192, 7], P(None, 'context'), may hold values from -2 to 2
Outputs:
- mixed: bfloat16 [4, 1024, 8192], P('dp', 'context')
- grad_q: bfloat16 [4, 1024, 8192], P('dp', 'context')
- grad_k: bfloat16 [4, 1024, 8192], P('dp', 'context')
- grad_v: bfloat16 [4, 1024, 8192], P('dp', 'context')
- grad_med: float32 [8192, 128], P('context', 'dp')
- grad_short: float32 [3, 8192, 7], P(None, 'context')
All inputs are finite; a program needn't handle non-finite values.
Results may differ from a plain program's by a relative error of at most 0.0058.
Values may be sent and summed in bfloat16 or wider, within the bound.
A program may use at most 384 MiB of HBM per device.

v0:
```python
import jax
import jax.numpy as jnp
from jax import lax
from jax.sharding import PartitionSpec as P


def short_forward(rows, before, taps):
    width = taps.shape[1]
    count = rows.shape[1]
    padded = jnp.concatenate([before, rows], axis=1).astype(jnp.float32)
    total = jnp.zeros(rows.shape, jnp.float32)
    for offset in range(width):
        start = width - 1 - offset
        total = total + taps[:, offset : offset + 1] * padded[:, start : start + count]
    return total


def short_backward(grads, after, taps):
    width = taps.shape[1]
    count = grads.shape[1]
    padded = jnp.concatenate([grads, after], axis=1)
    total = jnp.zeros(grads.shape, jnp.float32)
    for offset in range(width):
        total = total + taps[:, offset : offset + 1] * padded[:, offset : offset + count]
    return total


def short_weight(grads, rows, before):
    width = before.shape[1] + 1
    count = rows.shape[1]
    padded = jnp.concatenate([before, rows], axis=1).astype(jnp.float32)
    columns = []
    for offset in range(width):
        start = width - 1 - offset
        columns.append(jnp.sum(grads * padded[:, start : start + count], axis=1))
    return jnp.stack(columns, axis=1)


def band_table(size):
    shape = (size, 2 * size * size)
    tap = lax.broadcasted_iota(jnp.int32, shape, 0)
    place = lax.broadcasted_iota(jnp.int32, shape, 1)
    outpos = place // (2 * size)
    inpos = place % (2 * size)
    return (outpos + size - inpos == tap).astype(jnp.float32)


def toeplitz(taps, table):
    size = taps.shape[1]
    flat = jnp.dot(taps, table.astype(jnp.bfloat16), preferred_element_type=jnp.bfloat16)
    return flat.reshape(taps.shape[0], size, 2 * size)


def windows(rows, before):
    size = before.shape[1] + 1
    chans = rows.shape[0]
    first = jnp.concatenate([jnp.zeros((chans, 1), rows.dtype), before], axis=1)
    blocks = rows.reshape(chans, rows.shape[1] // size, size)
    earlier = jnp.concatenate([first[:, None], blocks[:, :-1]], axis=1)
    return jnp.concatenate([earlier, blocks], axis=2)


def medium_conv(rows, before, toep):
    frames = windows(rows, before)
    out = jnp.einsum("cbr,csr->cbs", frames, toep, preferred_element_type=jnp.float32)
    return out.reshape(rows.shape)


def medium_weight(grads, rows, before, table):
    size = before.shape[1] + 1
    chans = rows.shape[0]
    frames = windows(rows, before)
    blocks = grads.reshape(chans, -1, size)
    outer = jnp.einsum("cbs,cbr->csr", blocks, frames, preferred_element_type=jnp.float32)
    flat = outer.reshape(chans, 2 * size * size)
    return jnp.einsum(
        "cq,jq->cj",
        flat,
        table,
        precision=lax.Precision.HIGHEST,
        preferred_element_type=jnp.float32,
    )


def channel_forward(query, keys, values, htaps, shorts, table):
    chans = query.shape[0]
    rim_short = jnp.zeros((chans, shorts.shape[2] - 1), jnp.bfloat16)
    rim_med = jnp.zeros((chans, htaps.shape[1] - 1), jnp.bfloat16)
    toep = toeplitz(htaps, table)
    q_short = short_forward(query, rim_short, shorts[0])
    k_short = short_forward(keys, rim_short, shorts[1])
    v_short = short_forward(values, rim_short, shorts[2])
    product = (k_short * v_short).astype(jnp.bfloat16)
    conv_out = medium_conv(product, rim_med, toep)
    mixed = (q_short * conv_out).astype(jnp.bfloat16)
    saved = (
        query,
        keys,
        values,
        q_short,
        k_short,
        v_short,
        product,
        conv_out,
        toep,
        rim_short,
        rim_med,
    )
    return (mixed, saved)


def channel_backward(saved, cotangent, shorts, table):
    query, keys, values, q_short, k_short, v_short, product, conv_out, toep, rim_short, rim_med = (
        saved
    )
    after_short = jnp.zeros(rim_short.shape, jnp.float32)
    grad_f = cotangent.astype(jnp.float32)
    grad_z = (grad_f * q_short).astype(jnp.bfloat16)
    grad_qs = grad_f * conv_out
    grad_u = jnp.flip(medium_conv(jnp.flip(grad_z, 1), rim_med, toep), 1)
    grad_ks = grad_u * v_short
    grad_vs = grad_u * k_short
    grad_q = short_backward(grad_qs, after_short, shorts[0]).astype(jnp.bfloat16)
    grad_k = short_backward(grad_ks, after_short, shorts[1]).astype(jnp.bfloat16)
    grad_v = short_backward(grad_vs, after_short, shorts[2]).astype(jnp.bfloat16)
    grad_med = medium_weight(grad_z, product, rim_med, table)
    grad_short = jnp.stack(
        [
            short_weight(grad_qs, query, rim_short),
            short_weight(grad_ks, keys, rim_short),
            short_weight(grad_vs, values, rim_short),
        ],
        axis=0,
    )
    return (grad_q, grad_k, grad_v, grad_med, grad_short)


def to_tokens(rows):
    return rows.T[None]


def per_device(query_in, key_in, value_in, grad_out, med_filter, short_filter):
    htaps = lax.all_gather(med_filter.astype(jnp.bfloat16), "dp", axis=1, tiled=True)
    table = band_table(htaps.shape[1])
    query, keys, values = (
        lax.all_to_all(query_in, "context", split_axis=2, concat_axis=1, tiled=True),
        lax.all_to_all(key_in, "context", split_axis=2, concat_axis=1, tiled=True),
        lax.all_to_all(value_in, "context", split_axis=2, concat_axis=1, tiled=True),
    )
    mixed_c, saved = channel_forward(query[0].T, keys[0].T, values[0].T, htaps, short_filter, table)
    mixed = lax.all_to_all(to_tokens(mixed_c), "context", split_axis=1, concat_axis=2, tiled=True)
    cotangent = lax.all_to_all(grad_out, "context", split_axis=2, concat_axis=1, tiled=True)
    grad_qc, grad_kc, grad_vc, med_block, short_block = channel_backward(
        saved, cotangent[0].T, short_filter, table
    )
    grad_q, grad_k, grad_v = (
        lax.all_to_all(to_tokens(grad_qc), "context", split_axis=1, concat_axis=2, tiled=True),
        lax.all_to_all(to_tokens(grad_kc), "context", split_axis=1, concat_axis=2, tiled=True),
        lax.all_to_all(to_tokens(grad_vc), "context", split_axis=1, concat_axis=2, tiled=True),
    )
    grad_med = lax.psum_scatter(med_block, "dp", scatter_dimension=1, tiled=True)
    grad_short = lax.psum(short_block, "dp")
    return (mixed, grad_q, grad_k, grad_v, grad_med, grad_short)


def solution(mesh):
    placed = (
        P("dp", "context", None),
        P("dp", "context", None),
        P("dp", "context", None),
        P("dp", "context", None),
        P("context", "dp"),
        P(None, "context", None),
    )
    return jax.shard_map(
        per_device,
        mesh=mesh,
        in_specs=placed,
        out_specs=(
            P("dp", "context", None),
            P("dp", "context", None),
            P("dp", "context", None),
            P("dp", "context", None),
            P("context", "dp"),
            P(None, "context", None),
        ),
        check_vma=False,
    )
```

profile of v0, /device:TPU:0, one launch (start us, length us, event | category | flops | bytes accessed | tf_op | source)
XLA Modules:
  0.0 1141.2 jit_solution(11929751665857609553)
XLA Ops:
  7.2 9.5 copy.61
  17.2 45.2 %reduce = bf16[8192,128]{1,0:T(8,128)(2,1)S(1)} reduce(bf16[8192,1,128]{2,1,0:T(2,128)(2,1)} %bitcast.164, bf16[]{:T(256)} %broadcast.79), dimensions={1}, to_apply=%bitcast.124.reduce_sub_computation | reduce | bytes 4194306
  82.3 46.5 %reduce.1 = bf16[8192,128]{1,0:T(8,128)(2,1)} reduce(bf16[8192,1,128]{2,1,0:T(2,128)(2,1)} %bitcast.176, bf16[]{:T(256)} %broadcast.79), dimensions={1}, to_apply=%bitcast.128.reduce_sub_computation | reduce | bytes 4194306
  150.4 46.5 %reduce.2 = bf16[8192,128]{1,0:T(8,128)(2,1)} reduce(bf16[8192,1,128]{2,1,0:T(2,128)(2,1)} %bitcast.177, bf16[]{:T(256)} %broadcast.79), dimensions={1}, to_apply=%bitcast.126.reduce_sub_computation | reduce | bytes 4194306
  218.2 46.5 %reduce.3 = bf16[8192,128]{1,0:T(8,128)(2,1)} reduce(bf16[8192,1,128]{2,1,0:T(2,128)(2,1)} %bitcast.178, bf16[]{:T(256)} %broadcast.79), dimensions={1}, to_apply=%bitcast.132.reduce_sub_computation | reduce | bytes 4194306
  282.9 25.5 %fusion = bf16[32768,1024]{1,0:T(8,128)(2,1)} fusion(bf16[1024,128]{0,1:T(8,128)(2,1)S(1)} %all_gather.3, s32[32768]{0:T(1024)S(1)} %get-tuple-element.66, s32[32768]{0:T(1024)S(1)} %get-tuple-element.67, s32[32768]{0:T(1024)S(1)} %get-tuple-element.65, s32[32768]{0:T(1024)S(1)} %get-tuple-element.68, pred[32768]{0:T(1024)(128)(4,1)S(1)} %get-tuple-element.69, ...), kind=kOutput, calls=%fused_computation.2 | convolution fusion | flops 8619294720 | bytes 67960832 | tf_op jit(solution)/shard_map/dot_general | solution.py:50
  308.4 88.8 %copy.68 = bf16[1024,128,256]{2,1,0:T(8,128)(2,1)} copy(bf16[1024,128,256]{0,2,1:T(8,128)(2,1)} %bitcast.35) | data formatting | bytes 134217728 | tf_op jit(solution)/shard_map/reshape | solution.py:51
  460.5 15.4 %fusion.11 = (bf16[1024,1024]{0,1:T(8,128)(2,1)S(1)}, f32[1024,1024]{0,1:T(8,128)}) fusion(f32[1,128,8,1024]{3,1,2,0:T(8,128)} %copy.73, f32[1024,1030]{0,1:T(8,128)} %pad_convert_fusion.2, f32[1024]{0:T(1024)S(1)} %bitcast.231, f32[1024]{0:T(1024)S(1)} %bitcast.233, f32[1024]{0:T(1024)S(1)} %bitcast.235, f32[1024]{0:T(1024)S(1)} %bitcast.237, ...), kind=kLoop, calls=%fused_computation.16 | loop fusion | flops 15728640 | bytes 39874560 | tf_op jit(solution)/shard_map/convert_element_type | solution.py:118
  475.9 20.9 %rev.8 = bf16[1024,1024]{0,1:T(8,128)(2,1)} reverse(bf16[1024,1024]{0,1:T(8,128)(2,1)S(1)} %get-tuple-element.38), dimensions={1} | reverse | bytes 4194304 | tf_op jit(solution)/shard_map/jit(_flip)/rev | solution.py:120
  500.2 27.6 %fusion.5 = f32[1024,8,128]{2,1,0:T(8,128)} fusion(bf16[1024,128,256]{2,1,0:T(8,128)(2,1)} %copy.68, bf16[1024,7,128]{2,1,0:T(8,128)(2,1)S(1)} %bitcast.162, bf16[1024,8,128]{2,1,0:T(8,128)(2,1)S(1)} %copy.90), kind=kOutput, calls=%fused_computation.8 | convolution fusion | flops 549453824 | bytes 75235328 | tf_op jit(solution)/shard_map/cbr,csr->cbs/dot_general | solution.py:65
  533.2 32.8 %rev.9 = f32[1024,1024]{0,1:T(8,128)} reverse(f32[1024,1024]{0,1:T(8,128)} %bitcast.180), dimensions={1} | reverse | bytes 8388608 | tf_op jit(solution)/shard_map/jit(_flip)/rev | solution.py:120
  594.5 27.4 %fusion.18 = f32[1024,8,128]{2,1,0:T(8,128)} fusion(bf16[1024,128,256]{2,1,0:T(8,128)(2,1)} %copy.68, bf16[1024,7,128]{2,1,0:T(8,128)(2,1)S(1)} %bitcast.160, bf16[1024,8,128]{2,1,0:T(8,128)(2,1)S(1)} %copy.89), kind=kOutput, calls=%fused_computation.53 | convolution fusion | flops 549453824 | bytes 75235328 | tf_op jit(solution)/shard_map/cbr,csr->cbs/dot_general | solution.py:65
  627.4 18.3 %multiply_reduce_fusion.14 = (f32[1024]{0:T(1024)S(1)}, f32[1024]{0:T(1024)S(1)}, f32[1024]{0:T(1024)S(1)}, f32[1024]{0:T(1024)S(1)}, f32[1024]{0:T(1024)S(1)}, ...) fusion(f32[1024,1030]{0,1:T(8,128)} %pad_convert_fusion.2, ...), kind=kLoop, calls=%fused_computation.31 | loop fusion | flops 17818624 | bytes 48263168 | tf_op jit(solution)/shard_map/reduce_sum | solution.py:35
  650.9 14.1 %reduce.4 = bf16[1024,1024]{1,0:T(8,128)(2,1)} reduce(bf16[1024,1,1024]{2,1,0:T(2,128)(2,1)} %bitcast.169, bf16[]{:T(256)} %broadcast.79), dimensions={1}, to_apply=%bitcast.157.reduce_sub_computation | reduce | bytes 4194306
  677.7 12.7 %fusion.13 = bf16[1,1024,1024]{2,1,0:T(8,128)(2,1)S(1)} fusion(f32[1024]{0:T(1024)S(1)} %bitcast.232, f32[1024]{0:T(1024)S(1)} %bitcast.234, f32[1024]{0:T(1024)S(1)} %bitcast.236, f32[1024]{0:T(1024)S(1)} %bitcast.238, f32[1024]{0:T(1024)S(1)} %bitcast.240, f32[1024,1024]{0,1:T(8,128)} %get-tuple-element.33, f32[1024]{0:T(1024)S(1)} %bitcast.242, ...), kind=kLoop, calls=%fused_computation.49 | loop fusion | flops 14680064 | bytes 6320128 | tf_op jit(solution)/shard_map/broadcast_in_dim | solution.py:139
  695.6 14.1 %reduce.5 = bf16[1024,1024]{1,0:T(8,128)(2,1)} reduce(bf16[1024,1,1024]{2,1,0:T(2,128)(2,1)} %bitcast.170, bf16[]{:T(256)} %broadcast.79), dimensions={1}, to_apply=%bitcast.156.reduce_sub_computation | reduce | bytes 4194306
  716.0 10.0 all-to-all-done.3
  730.5 12.8 %fusion.14 = bf16[1,1024,1024]{2,1,0:T(8,128)(2,1)S(1)} fusion(f32[1024]{0:T(1024)S(1)} %bitcast.226, f32[1024]{0:T(1024)S(1)} %bitcast.224, f32[1024]{0:T(1024)S(1)} %bitcast.222, f32[1024]{0:T(1024)S(1)} %bitcast.220, f32[1024]{0:T(1024)S(1)} %bitcast.218, f32[1024,1024]{0,1:T(8,128)} %get-tuple-element.34, f32[1024]{0:T(1024)S(1)} %bitcast.216, ...), kind=kLoop, calls=%fused_computation.50 | loop fusion | flops 14680064 | bytes 6320128 | tf_op jit(solution)/shard_map/broadcast_in_dim | solution.py:139
  748.4 14.1 %reduce.6 = bf16[1024,1024]{1,0:T(8,128)(2,1)} reduce(bf16[1024,1,1024]{2,1,0:T(2,128)(2,1)} %bitcast.171, bf16[]{:T(256)} %broadcast.79), dimensions={1}, to_apply=%bitcast.155.reduce_sub_computation | reduce | bytes 4194306
  768.7 12.9 %fusion.15 = bf16[1,1024,1024]{2,1,0:T(8,128)(2,1)S(1)} fusion(f32[1024]{0:T(1024)S(1)} %bitcast.204, f32[1024]{0:T(1024)S(1)} %bitcast.206, f32[1024]{0:T(1024)S(1)} %bitcast.208, f32[1024]{0:T(1024)S(1)} %bitcast.210, f32[1024]{0:T(1024)S(1)} %bitcast.212, f32[1024,1024]{0,1:T(8,128)} %get-tuple-element.36, f32[1024]{0:T(1024)S(1)} %bitcast.214, ...), kind=kLoop, calls=%fused_computation.51 | loop fusion | flops 14680064 | bytes 6320128 | tf_op jit(solution)/shard_map/broadcast_in_dim | solution.py:139
  786.8 14.1 %reduce.7 = bf16[1024,1024]{1,0:T(8,128)(2,1)} reduce(bf16[1024,1,1024]{2,1,0:T(2,128)(2,1)} %bitcast.165, bf16[]{:T(256)} %broadcast.79), dimensions={1}, to_apply=%bitcast.154.reduce_sub_computation | reduce | bytes 4194306
  817.3 46.6 %fusion.16 = f32[1024,128,256]{2,1,0:T(8,128)} fusion(bf16[1024,8,128]{2,1,0:T(8,128)(2,1)} %copy.84, bf16[1024,7,128]{2,1,0:T(8,128)(2,1)S(1)} %bitcast.161, bf16[1024,8,128]{2,1,0:T(8,128)(2,1)S(1)} %copy.89), kind=kOutput, calls=%fused_computation.52 | convolution fusion | flops 549453824 | bytes 140247040 | tf_op jit(solution)/shard_map/cbs,cbr->csr/dot_general | solution.py:74
  864.0 108.5 %copy.100 = f32[128,8,128,256]{3,1,2,0:T(8,128)} copy(f32[128,8,128,256]{3,2,1,0:T(8,128)} %bitcast.108) | data formatting | bytes 268435456
  979.7 81.5 %fusion.35 = f32[1024,128]{0,1:T(8,128)} fusion(f32[1024,32768]{1,0:T(8,128)} %bitcast.109, s32[32768]{0:T(1024)S(1)} %copy-done.6, s32[32768]{0:T(1024)S(1)} %copy-done.8, s32[32768]{0:T(1024)S(1)} %copy-done.4, s32[32768]{0:T(1024)S(1)} %copy-done.10, pred[32768]{0:T(1024)(128)(4,1)S(1)} %copy-done.12, pred[32768]{0:T(1024)(128)(4,1)S(1)} %copy-done.14), kind=kOutput, calls=%fused_computation.77 | convolution fusion | flops 51560579072 | bytes 135331840 | tf_op jit(solution)/shard_map/cq,jq->cj/dot_general | solution.py:76
  (150 shorter events, 334.1 us)
Async XLA Ops:
  65.6 69.0 %all-to-all-start = ((bf16[8,2,65536]{2,1,0:T(2,128)(2,1)}), bf16[8,2,65536]{2,1,0:T(2,128)(2,1)S(1)}, u32[]{:S(2)}, u32[]{:S(2)}) async-start(bf16[8,2,65536]{2,1,0:T(2,128)(2,1)} %reshape.52), calls=%async_computation | async-start | bytes 4194304 | tf_op jit(solution)/shard_map/all_to_all | solution.py:146
  134.6 68.1 %all-to-all-start.2 = ((bf16[8,2,65536]{2,1,0:T(2,128)(2,1)}), bf16[8,2,65536]{2,1,0:T(2,128)(2,1)}, u32[]{:S(2)}, u32[]{:S(2)}) async-start(bf16[8,2,65536]{2,1,0:T(2,128)(2,1)} %reshape.56), calls=%async_computation.2 | async-start | bytes 4194304 | tf_op jit(solution)/shard_map/all_to_all | solution.py:148
  202.7 73.7 %all-to-all-start.1 = ((bf16[8,2,65536]{2,1,0:T(2,128)(2,1)}), bf16[8,2,65536]{2,1,0:T(2,128)(2,1)}, u32[]{:S(2)}, u32[]{:S(2)}) async-start(bf16[8,2,65536]{2,1,0:T(2,128)(2,1)} %reshape.54), calls=%async_computation.1 | async-start | bytes 4194304 | tf_op jit(solution)/shard_map/all_to_all | solution.py:147
  276.4 163.5 %all-to-all-start.4 = ((bf16[8,2,65536]{2,1,0:T(2,128)(2,1)}), bf16[8,2,65536]{2,1,0:T(2,128)(2,1)}, u32[]{:S(2)}, u32[]{:S(2)}) async-start(bf16[8,2,65536]{2,1,0:T(2,128)(2,1)} %reshape.60), calls=%async_computation.4 | async-start | bytes 4194304 | tf_op jit(solution)/shard_map/all_to_all | solution.py:152
  671.2 54.7 %all-to-all-start.3 = ((bf16[8,2,65536]{2,1,0:T(2,128)(2,1)}), bf16[8,2,65536]{2,1,0:T(2,128)(2,1)}, u32[]{:S(2)}, u32[]{:S(2)}) async-start(bf16[8,2,65536]{2,1,0:T(2,128)(2,1)} %reshape.58), calls=%async_computation.3 | async-start | bytes 4194304 | tf_op jit(solution)/shard_map/all_to_all | solution.py:151
  725.9 85.4 %all-to-all-start.5 = ((bf16[8,2,65536]{2,1,0:T(2,128)(2,1)}), bf16[8,2,65536]{2,1,0:T(2,128)(2,1)}, u32[]{:S(2)}, u32[]{:S(2)}) async-start(bf16[8,2,65536]{2,1,0:T(2,128)(2,1)} %reshape.62), calls=%async_computation.5 | async-start | bytes 4194304 | tf_op jit(solution)/shard_map/all_to_all | solution.py:157
  811.3 162.3 %all-to-all-start.6 = ((bf16[8,2,65536]{2,1,0:T(2,128)(2,1)}), bf16[8,2,65536]{2,1,0:T(2,128)(2,1)}, u32[]{:S(2)}, u32[]{:S(2)}) async-start(bf16[8,2,65536]{2,1,0:T(2,128)(2,1)} %reshape.64), calls=%async_computation.6 | async-start | bytes 4194304 | tf_op jit(solution)/shard_map/all_to_all | solution.py:158
  817.3 315.1 %all-reduce.10.cloned.1.call-start = ((), (), s32[]{:S(2)}) async-start(), calls=%async_computation.10 | async-start | bytes 196608 | tf_op jit(solution)/shard_map/psum | solution.py:162
  863.9 108.7 %copy-start.17 = (f32[1024]{0:T(1024)S(1)}, f32[1024]{0:T(1024)}, u32[]{:S(2)}) copy-start(f32[1024]{0:T(1024)} %get-tuple-element.26) | copy-start | bytes 12292
  863.9 108.7 %copy-start.18 = (f32[1024]{0:T(1024)S(1)}, f32[1024]{0:T(1024)}, u32[]{:S(2)}) copy-start(f32[1024]{0:T(1024)} %get-tuple-element.27) | copy-start | bytes 12292
  863.9 108.7 %copy-start.19 = (f32[1024]{0:T(1024)S(1)}, f32[1024]{0:T(1024)}, u32[]{:S(2)}) copy-start(f32[1024]{0:T(1024)} %get-tuple-element.28) | copy-start | bytes 12292
  863.9 108.7 %copy-start.20 = (f32[1024]{0:T(1024)S(1)}, f32[1024]{0:T(1024)}, u32[]{:S(2)}) copy-start(f32[1024]{0:T(1024)} %get-tuple-element.29) | copy-start | bytes 12292
  863.9 108.7 %copy-start.21 = (f32[1024]{0:T(1024)S(1)}, f32[1024]{0:T(1024)}, u32[]{:S(2)}) copy-start(f32[1024]{0:T(1024)} %get-tuple-element.30) | copy-start | bytes 12292
  863.9 108.7 %copy-start.22 = (f32[1024]{0:T(1024)S(1)}, f32[1024]{0:T(1024)}, u32[]{:S(2)}) copy-start(f32[1024]{0:T(1024)} %get-tuple-element.31) | copy-start | bytes 12292
  863.9 108.7 %copy-start.23 = (f32[1024]{0:T(1024)S(1)}, f32[1024]{0:T(1024)}, u32[]{:S(2)}) copy-start(f32[1024]{0:T(1024)} %get-tuple-element.32) | copy-start | bytes 12292
  863.9 108.8 %copy-start.24 = (f32[1024]{0:T(1024)S(1)}, f32[1024]{0:T(1024)}, u32[]{:S(2)}) copy-start(f32[1024]{0:T(1024)} %get-tuple-element.19) | copy-start | bytes 12292
  863.9 108.8 %copy-start.25 = (f32[1024]{0:T(1024)S(1)}, f32[1024]{0:T(1024)}, u32[]{:S(2)}) copy-start(f32[1024]{0:T(1024)} %get-tuple-element.20) | copy-start | bytes 12292
  863.9 108.8 %copy-start.26 = (f32[1024]{0:T(1024)S(1)}, f32[1024]{0:T(1024)}, u32[]{:S(2)}) copy-start(f32[1024]{0:T(1024)} %get-tuple-element.21) | copy-start | bytes 12292
  863.9 108.8 %copy-start.27 = (f32[1024]{0:T(1024)S(1)}, f32[1024]{0:T(1024)}, u32[]{:S(2)}) copy-start(f32[1024]{0:T(1024)} %get-tuple-element.22) | copy-start | bytes 12292
  864.0 108.8 %copy-start.28 = (f32[1024]{0:T(1024)S(1)}, f32[1024]{0:T(1024)}, u32[]{:S(2)}) copy-start(f32[1024]{0:T(1024)} %get-tuple-element.23) | copy-start | bytes 12292
  864.0 108.8 %copy-start.29 = (f32[1024]{0:T(1024)S(1)}, f32[1024]{0:T(1024)}, u32[]{:S(2)}) copy-start(f32[1024]{0:T(1024)} %get-tuple-element.24) | copy-start | bytes 12292
  864.0 108.8 %copy-start.30 = (f32[1024]{0:T(1024)S(1)}, f32[1024]{0:T(1024)}, u32[]{:S(2)}) copy-start(f32[1024]{0:T(1024)} %get-tuple-element.25) | copy-start | bytes 12292
  973.6 144.9 %all-to-all-start.7 = ((bf16[8,2,65536]{2,1,0:T(2,128)(2,1)}), bf16[8,2,65536]{2,1,0:T(2,128)(2,1)S(1)}, u32[]{:S(2)}, u32[]{:S(2)}) async-start(bf16[8,2,65536]{2,1,0:T(2,128)(2,1)} %reshape.66), calls=%async_computation.7 | async-start | bytes 4194304 | tf_op jit(solution)/shard_map/all_to_all | solution.py:159
  979.6 152.8 %reduce-scatter.2.cloned.1.call-start = ((), (), s32[]{:S(2)}) async-start(), calls=%async_computation.9 | async-start | bytes 655360 | tf_op jit(solution)/shard_map/reduce_scatter | solution.py:161
  (17 other events, 391.9 us)
Sparse Core Ops, SparseCore 0:
  973.7 32.7 all-reduce.9
  1061.3 23.0 reduce-scatter.1
where the time goes:
time: 1160 us; the launch traced here: 1140 us
  local copies, waits for them, and re-layouts  503 us (43%)
  other arithmetic  350 us (30%)
  matrix products  209 us (18%)
  starting transfers between devices  49 us (4%)
  between operations  15.1 us (1%)
    unnamed x96, local copies, waits for them, and re-layouts  288 us
    unnamed x8, other arithmetic  241 us
    reshape x1, local copies, waits for them, and re-layouts, toeplitz(): return flat.reshape(taps.shape[0], size, 2 * size)  88.8 us
    dot_general x1, matrix products, medium_weight(): jnp.einsum('cq,jq->cj', flat, table, precision=lax.Precision.HIGHEST, pre...  81.5 us
    dot_general x2, matrix products, medium_conv(): jnp.einsum('cbr,csr->cbs', frames, toep, preferred_element_type=jnp.float32)  55 us
    rev x2, local copies, waits for them, and re-layouts, channel_backward(): grad_u = jnp.flip(medium_conv(jnp.flip(grad_z, 1), rim_med, toep), 1)  53.6 us
    dot_general x1, matrix products, medium_weight(): jnp.einsum('cbs,cbr->csr', blocks, frames, preferred_element_type=jnp.flo...  46.6 us
    broadcast_in_dim x3, other arithmetic, to_tokens(): return rows.T[None]  38.3 us
  transfers between devices with their start and end apart: 10, of which 1 were waited for; matrix products, arithmetic and copies ran while one was open for 67% of the time, Pallas kernels for 0%

commit v1 on v0

v1 whole, which is shorter than its diff:
```python
import functools

import numpy as np
import jax
import jax.numpy as jnp
from jax import lax
from jax.experimental import pallas as pl
from jax.experimental.pallas import tpu as pltpu
from jax.sharding import PartitionSpec as P

HALO = 8
BF = jnp.bfloat16
F32 = jnp.float32


def split_np(x):
    hi = x.astype(np.float32).astype(BF)
    lo = (x - hi.astype(np.float64)).astype(np.float32).astype(BF)
    return hi, lo


def tables(length):
    size = 2 * length
    theta = np.pi * (2 * np.arange(length) + 1)[:, None] / size

    def forward(places):
        angle = theta * places[None, :]
        hi, lo = split_np(np.concatenate([np.cos(angle), -np.sin(angle)], axis=0))
        return np.concatenate([hi, lo], axis=1)

    def inverse(places):
        angle = theta * places[None, :]
        both = np.concatenate([np.cos(angle), -np.sin(angle)], axis=0).T * (2.0 / size)
        hi, lo = split_np(both)
        return np.concatenate([hi, lo], axis=0)

    n = np.arange(length)
    return np.stack([forward(n), forward(n + length), inverse(n + length), inverse(n), inverse(n - length)])


def dot(a, b):
    return jnp.dot(a, b, preferred_element_type=F32)


def short_conv(pad_ref, taps, width, count):
    total = taps[0:1] * pad_ref[pl.ds(HALO, count)]
    for j in range(1, width):
        total = total + taps[j : j + 1] * pad_ref[pl.ds(HALO - j, count)]
    return total


def first_kernel(width, q_ref, k_ref, v_ref, g_ref, halo_ref, s_ref, u_ref, d_ref, pad_ref):
    count = q_ref.shape[0]

    def conv(i, ref):
        pad_ref[0:HALO] = halo_ref[i].astype(F32)
        pad_ref[HALO:] = ref[...].astype(F32)
        return short_conv(pad_ref, s_ref[i], width, count)

    ks = conv(1, k_ref)
    u_ref[...] = (ks * conv(2, v_ref)).astype(BF)
    d_ref[...] = (g_ref[...].astype(F32) * conv(0, q_ref)).astype(BF)


def second_kernel(width, *refs):
    q_ref, k_ref, v_ref, g_ref, halo_ref, s_ref, uo_ref, up_ref, do_ref, dn_ref, h_ref, tab_ref = refs[:12]
    mixed_ref, gq_ref, gk_ref, gv_ref, acc_ref, head_ref, tail_ref = refs[-11:-4]
    padq, padk, padv, padg = refs[-4:]
    length = q_ref.shape[0]
    chans = q_ref.shape[1]

    def double(x):
        return jnp.concatenate([x, x], axis=0)

    wave = dot(tab_ref[0], double(up_ref[...])) + dot(tab_ref[1], double(uo_ref[...]))
    own = dot(tab_ref[0], double(do_ref[...]))
    ahead = own + dot(tab_ref[1], double(dn_ref[...]))
    filt = dot(tab_ref[0], double(h_ref[...].reshape(length, chans)))

    def times(a, b, sign):
        ar, ai = a[:length], a[length:]
        br, bi = b[:length], b[length:]
        if sign > 0:
            return jnp.concatenate([ar * br - ai * bi, ar * bi + ai * br], axis=0)
        return jnp.concatenate([ar * br + ai * bi, ai * br - ar * bi], axis=0)

    def back(spectrum, index):
        hi = spectrum.astype(BF)
        lo = (spectrum - hi.astype(F32)).astype(BF)
        both = dot(tab_ref[index], hi)
        return both[:length] + both[length:] + dot(tab_ref[index, :length], lo)

    z = back(times(wave, filt, 1), 2)
    du = back(times(ahead, filt, -1), 3)
    gm = back(times(own, wave, -1), 4)

    parts = acc_ref.shape[0]
    share = length // parts
    acc_ref[:, 0, :share] = gm.reshape(parts, share, chans)
    acc_ref[:, 0, share:] = jnp.zeros((parts, acc_ref.shape[2] - share, chans), F32)

    def load(i, ref, pad):
        pad[0:HALO] = halo_ref[i].astype(F32)
        pad[HALO:] = ref[...].astype(F32)
        return short_conv(pad, s_ref[i], width, length)

    padg[0:HALO] = jnp.zeros((HALO, chans), F32)
    padg[HALO + length :] = jnp.zeros((HALO, chans), F32)

    def finish(i, grads, pad, out_ref):
        padg[HALO : HALO + length] = grads
        taps = s_ref[i]
        total = taps[0:1] * grads
        head = taps[1:2] * padg[1 : 1 + HALO]
        sums = [jnp.sum(grads * pad[HALO : HALO + length], axis=0, keepdims=True)]
        for j in range(1, width):
            total = total + taps[j : j + 1] * padg[pl.ds(HALO + j, length)]
            if j > 1:
                head = head + taps[j : j + 1] * padg[j : j + HALO]
            sums.append(jnp.sum(grads * pad[pl.ds(HALO - j, length)], axis=0, keepdims=True))
        out_ref[...] = total.astype(BF)
        head_ref[i] = head.astype(BF)
        tail_ref[i] = total[length - HALO :]
        slot = acc_ref.shape[2] - share
        row = i * HALO
        acc_ref[row // slot, 0, pl.ds(share + row % slot, width)] = jnp.concatenate(sums, axis=0)

    qs = load(0, q_ref, padq)
    mixed_ref[...] = (qs * z).astype(BF)
    finish(0, g_ref[...].astype(F32) * z, padq, gq_ref)
    ks = load(1, k_ref, padk)
    vs = load(2, v_ref, padv)
    finish(1, du * vs, padk, gk_ref)
    finish(2, du * ks, padv, gv_ref)


def per_device(n_dp, n_ctx, query_in, key_in, value_in, grad_out, med_filter, short_filter):
    q, k, v, g = (a[0] for a in (query_in, key_in, value_in, grad_out))
    length, full = q.shape
    width = short_filter.shape[2]
    chans = full // n_ctx
    share = med_filter.shape[1]
    pieces = max(1, min(4, chans // 128))
    part = chans // pieces
    cb = 256 if part % 256 == 0 else 128
    inner = part // cb
    slot = HALO * (-(-3 // n_dp))
    right = [(i, i + 1) for i in range(n_ctx - 1)]
    left = [(i + 1, i) for i in range(n_ctx - 1)]
    assert n_dp * share == length and width - 1 <= HALO

    shorts = jnp.pad(short_filter.transpose(0, 2, 1), ((0, 0), (0, HALO - width), (0, 0)))
    shorts = lax.all_gather(shorts, "context")
    taps = lax.all_gather(med_filter.astype(BF).T, "context")
    taps = lax.all_gather(taps, "dp")
    table = jnp.asarray(tables(length))

    rim = jnp.stack([a[length - HALO :] for a in (q, k, v)])
    rim = rim.reshape(3, HALO, n_ctx, pieces, part)
    rims = [lax.ppermute(rim[:, :, :, c].reshape(3, HALO, n_ctx * part), "context", right) for c in range(pieces)]

    def whole(c):
        return pl.BlockSpec((length, cb), lambda b, i: (0, b * (chans // cb) + c * inner + i))

    piece = pl.BlockSpec((length, cb), lambda b, i: (0, b * inner + i))
    rim_spec = pl.BlockSpec((3, HALO, cb), lambda b, i: (0, 0, b * inner + i))

    def short_spec(c):
        return pl.BlockSpec((pl.squeezed, 3, HALO, cb), lambda b, i: (b, 0, 0, c * inner + i))

    sent = []
    for c in range(pieces):
        sent.append(
            pl.pallas_call(
                functools.partial(first_kernel, width),
                grid=(n_ctx, inner),
                in_specs=[whole(c)] * 4 + [rim_spec, short_spec(c)],
                out_specs=[piece] * 2,
                out_shape=[jax.ShapeDtypeStruct((length, n_ctx * part), BF)] * 2,
                scratch_shapes=[pltpu.VMEM((HALO + length, cb), F32)],
                cost_estimate=pl.CostEstimate(
                    flops=50 * length * n_ctx * part, bytes_accessed=24 * length * n_ctx * part, transcendentals=0
                ),
                name="featurize",
            )(q, k, v, g, rims[c], shorts)
        )
    arrived = [
        (lax.ppermute(u, "context", right), lax.ppermute(d, "context", left)) for u, d in sent
    ]

    grown = None
    sums = []
    heads = []
    tails = []
    for c in range(pieces):
        tap_spec = pl.BlockSpec((n_dp, 1, share, cb), lambda b, i, c=c: (0, b, 0, c * inner + i))
        table_spec = pl.BlockSpec(table.shape, lambda b, i: (0, 0, 0))
        args = [q, k, v, g, rims[c], shorts, sent[c][0], arrived[c][0], sent[c][1], arrived[c][1], taps, table]
        specs = [whole(c)] * 4 + [rim_spec, short_spec(c)] + [piece] * 4 + [tap_spec, table_spec]
        alias = {}
        if grown is not None:
            alias = {len(args) + i: i for i in range(4)}
            args += grown
            specs += [pl.BlockSpec(memory_space=pl.ANY)] * 4
        outs = pl.pallas_call(
            functools.partial(second_kernel, width),
            grid=(n_ctx, inner),
            in_specs=specs,
            out_specs=[whole(c)] * 4
            + [pl.BlockSpec((n_dp, 1, share + slot, cb), lambda b, i: (0, b, 0, i)), rim_spec, rim_spec],
            out_shape=[jax.ShapeDtypeStruct((length, full), BF)] * 4
            + [
                jax.ShapeDtypeStruct((n_dp, n_ctx, share + slot, part), F32),
                jax.ShapeDtypeStruct((3, HALO, n_ctx * part), BF),
                jax.ShapeDtypeStruct((3, HALO, n_ctx * part), F32),
            ],
            scratch_shapes=[pltpu.VMEM((HALO + length, cb), F32)] * 3 + [pltpu.VMEM((2 * HALO + length, cb), F32)],
            input_output_aliases=alias,
            cost_estimate=pl.CostEstimate(
                flops=4000 * length * n_ctx * part, bytes_accessed=80 * length * n_ctx * part, transcendentals=0
            ),
            compiler_params=pltpu.CompilerParams(vmem_limit_bytes=48 * 1024 * 1024),
            name="mixer",
        )(*args)
        grown = list(outs[:4])
        total = lax.psum_scatter(outs[4], "dp", scatter_dimension=0)
        sums.append(lax.psum_scatter(total, "context", scatter_dimension=0))
        heads.append(lax.ppermute(outs[5], "context", left))
        tails.append(outs[6])

    def join(items):
        return jnp.concatenate([a.reshape(3, HALO, n_ctx, 1, part) for a in items], axis=3).reshape(3, HALO, full)

    fixed = (join(tails) + join(heads).astype(F32)).astype(BF)
    grads = [lax.dynamic_update_slice(a, fixed[i], (length - HALO, 0)) for i, a in enumerate(grown[1:])]
    total = jnp.concatenate(sums, axis=1)
    grad_med = total[:share].T
    short = lax.all_gather(total[share:], "dp", tiled=True)[: 3 * HALO]
    grad_short = short.reshape(3, HALO, chans)[:, :width].transpose(0, 2, 1)
    return (grown[0][None], grads[0][None], grads[1][None], grads[2][None], grad_med, grad_short)


def solution(mesh):
    rows = P("dp", "context", None)
    med = P("context", "dp")
    short = P(None, "context", None)
    return jax.shard_map(
        functools.partial(per_device, mesh.shape["dp"], mesh.shape["context"]),
        mesh=mesh,
        in_specs=(rows, rows, rows, rows, med, short),
        out_specs=(rows, rows, rows, rows, med, short),
        check_vma=False,
    )
```

time: 1160 us -> 624 us (0.54); the launches traced: 1140 us -> 621 us
  local copies, waits for them, and re-layouts: 503 us -> 6.92 us
  waiting for transfers between devices: 10 us -> 384 us
  other arithmetic: 350 us -> 2.79 us
  matrix products: 209 us -> 0 us
  Pallas kernels: 0 us -> 101 us
  blocking collectives: 5.77 us -> 74.4 us
    reduce_scatter x1 -> x8, waiting for transfers between devices: 0.01 us -> 355 us  [the longest x4 255 us: per_device(): sums.append(lax.psum_scatter(total, 'context', scatter_dimension=0))]
    unnamed x96 -> x54, local copies, waits for them, and re-layouts: 288 us -> 4.09 us
    unnamed x8 -> x0, other arithmetic: 241 us -> none
    dot_general x5 -> x0, matrix products: 209 us -> none  [the longest x1 81.5 us: medium_weight(): jnp.einsum('cq,jq->cj', flat, table, precision=lax.Precision.HIGHEST, pre...]
    reshape x6 -> x1, local copies, waits for them, and re-layouts: 111 us -> 0.01 us  [per_device(): grad_short = short.reshape(3, HALO, chans)[:, :width].transpose(0, 2, 1)]
    pallas_call x0 -> x8, Pallas kernels: none -> 101 us  [the longest x4 73.7 us: per_device(): pl.pallas_call(functools.partial(second_kernel, width), grid=(n_ctx, inne...]
    all_gather x1 -> x3, blocking collectives: 5.77 us -> 74.4 us  [the longest x1 35.2 us: per_device(): taps = lax.all_gather(med_filter.astype(BF).T, 'context')]
    rev x2 -> x0, local copies, waits for them, and re-layouts: 53.6 us -> none  [channel_backward(): grad_u = jnp.flip(medium_conv(jnp.flip(grad_z, 1), rim_med, toep), 1)]
  transfers between devices with their start and end apart: 10 -> 25, of which waited for: 1 -> 13; matrix products, arithmetic and copies ran while one was open for 67% -> 0% of each run, Pallas kernels for 0% -> 13%
where the time goes in v1:
time: 624 us; the launch traced here: 621 us
  waiting for transfers between devices  384 us (62%)
  Pallas kernels  101 us (16%)
  blocking collectives  74.4 us (12%)
  starting transfers between devices  38.2 us (6%)
  between operations  14.4 us (2%)
  local copies, waits for them, and re-layouts  6.92 us (1%)
    reduce_scatter x4, waiting for transfers between devices, per_device(): sums.append(lax.psum_scatter(total, 'context', scatter_dimension=0))  255 us
    reduce_scatter x4, waiting for transfers between devices, per_device(): total = lax.psum_scatter(outs[4], 'dp', scatter_dimension=0)  100 us
    pallas_call x4, Pallas kernels, per_device(): pl.pallas_call(functools.partial(second_kernel, width), grid=(n_ctx, inne...  73.7 us
    all_gather x1, blocking collectives, per_device(): taps = lax.all_gather(med_filter.astype(BF).T, 'context')  35.2 us
    all_gather x1, blocking collectives, per_device(): shorts = lax.all_gather(shorts, 'context')  33.7 us
    pallas_call x4, Pallas kernels, per_device(): pl.pallas_call(functools.partial(first_kernel, width), grid=(n_ctx, inner...  27.5 us
    ppermute x4, waiting for transfers between devices, per_device(): lax.ppermute(rim[:, :, :, c].reshape(3, HALO, n_ctx * part), 'context', r...  19.5 us
    ppermute x4, starting transfers between devices, per_device(): lax.ppermute(u, 'context', right)  15.4 us
  transfers between devices with their start and end apart: 25, of which 13 were waited for; matrix products, arithmetic and copies ran while one was open for 0% of the time, Pallas kernels for 13%

profile of v1, /device:TPU:0, one launch (start us, length us, event | category | flops | bytes accessed | tf_op | source)
XLA Modules:
  0.0 621.5 jit_solution(13379727351501692992)
XLA Ops:
  8.3 35.2 %all-gather.1 = bf16[256,1024]{1,0:T(8,128)(2,1)} all-gather(bf16[32,1024]{1,0:T(8,128)(2,1)S(1)} %convert_bitcast_fusion), channel_id=3, replica_groups=mesh['dp'=4,'context'=8] {'context'}, dimensions={0}, use_global_device_ids=true | all-gather | bytes 589824 | tf_op jit(solution)/shard_map/all_gather | solution.py:154
  43.7 3.5 collective-permute-start.9
  49.2 33.7 %all-gather = f32[24,8,1024]{2,1,0:T(8,128)} all-gather(f32[3,8,1024]{2,1,0:T(8,128)S(1)} %pad.4), channel_id=2, replica_groups=mesh['dp'=4,'context'=8] {'context'}, dimensions={0}, use_global_device_ids=true | all-gather | bytes 884736 | tf_op jit(solution)/shard_map/all_gather | solution.py:153
  83.6 6.8 %featurize.7 = (bf16[128,2048]{1,0:T(8,128)(2,1)}, bf16[128,2048]{1,0:T(8,128)(2,1)}) custom-call(bf16[128,8192]{1,0:T(8,128)(2,1)} %bitcast.66, bf16[128,8192]{1,0:T(8,128)(2,1)} %bitcast.75, bf16[128,8192]{1,0:T(8,128)(2,1)} %bitcast.84, bf16[128,8192]{1,0:T(8,128)(2,1)} %bitcast.93, bf16[3,8,2048]{2,1,0:T(8,128)(2,1)} %copy-done.12, ...), custom_call_target="tpu_custom_call" | custom-call | flops 13107200 | bytes 6291456 | tf_op jit(solution)/shard_map/featurize/pallas_call | solution.py:174
  95.2 6.9 %featurize.6 = (bf16[128,2048]{1,0:T(8,128)(2,1)}, bf16[128,2048]{1,0:T(8,128)(2,1)}) custom-call(bf16[128,8192]{1,0:T(8,128)(2,1)} %bitcast.67, bf16[128,8192]{1,0:T(8,128)(2,1)} %bitcast.76, bf16[128,8192]{1,0:T(8,128)(2,1)} %bitcast.85, bf16[128,8192]{1,0:T(8,128)(2,1)} %bitcast.94, bf16[3,8,2048]{2,1,0:T(8,128)(2,1)} %copy-done.14, ...), custom_call_target="tpu_custom_call" | custom-call | flops 13107200 | bytes 6291456 | tf_op jit(solution)/shard_map/featurize/pallas_call | solution.py:174
  102.0 5.4 collective-permute-start.7
  110.7 19.5 %collective-permute-done.3.halo_ref.refs_4_ = bf16[3,8,2048]{2,1,0:T(8,128)(2,1)S(1)} collective-permute-done((bf16[3,8,2048]{2,1,0:T(8,128)(2,1)S(1)}, bf16[3,8,2048]{2,1,0:T(8,128)(2,1)S(1)}, u32[]{:S(2)}, u32[]{:S(2)}) %collective-permute-start.3) | collective-permute-done | bytes 98336 | tf_op jit(solution)/shard_map/ppermute | solution.py:160
  130.1 4.4 collective-permute-start
  134.5 6.9 %featurize.5 = (bf16[128,2048]{1,0:T(8,128)(2,1)}, bf16[128,2048]{1,0:T(8,128)(2,1)}) custom-call(bf16[128,8192]{1,0:T(8,128)(2,1)} %bitcast.68, bf16[128,8192]{1,0:T(8,128)(2,1)} %bitcast.77, bf16[128,8192]{1,0:T(8,128)(2,1)} %bitcast.86, bf16[128,8192]{1,0:T(8,128)(2,1)} %bitcast.95, bf16[3,8,2048]{2,1,0:T(8,128)(2,1)} %copy-done.18, ...), custom_call_target="tpu_custom_call" | custom-call | flops 13107200 | bytes 6291456 | tf_op jit(solution)/shard_map/featurize/pallas_call | solution.py:174
  145.6 6.9 %featurize.4 = (bf16[128,2048]{1,0:T(8,128)(2,1)}, bf16[128,2048]{1,0:T(8,128)(2,1)}) custom-call(bf16[128,8192]{1,0:T(8,128)(2,1)} %bitcast.69, bf16[128,8192]{1,0:T(8,128)(2,1)} %bitcast.78, bf16[128,8192]{1,0:T(8,128)(2,1)} %bitcast.87, bf16[128,8192]{1,0:T(8,128)(2,1)} %bitcast.96, bf16[3,8,2048]{2,1,0:T(8,128)(2,1)} %copy-done.16, ...), custom_call_target="tpu_custom_call" | custom-call | flops 13107200 | bytes 6291456 | tf_op jit(solution)/shard_map/featurize/pallas_call | solution.py:174
  153.3 4.6 collective-permute-start.1
  161.4 18.4 %mixer.4 = (bf16[128,8192]{1,0:T(8,128)(2,1)}, bf16[128,8192]{1,0:T(8,128)(2,1)}, bf16[128,8192]{1,0:T(8,128)(2,1)}, bf16[128,8192]{1,0:T(8,128)(2,1)}, f32[4,8,...) custom-call(bf16[128,8192]{1,0:T(8,128)(2,1)} %bitcast.70, ...), custom_call_target="tpu_custom_call" | custom-call | flops 1048576000 | bytes 20971520 | tf_op jit(solution)/shard_map/mixer/pallas_call | solution.py:205
  179.9 18.4 %mixer.5 = (bf16[128,8192]{1,0:T(8,128)(2,1)}, bf16[128,8192]{1,0:T(8,128)(2,1)}, bf16[128,8192]{1,0:T(8,128)(2,1)}, bf16[128,8192]{1,0:T(8,128)(2,1)}, f32[4,8,...) custom-call(bf16[128,8192]{1,0:T(8,128)(2,1)} %bitcast.71, ...), custom_call_target="tpu_custom_call", output_to_operand_aliasing={{0}: (12, {}), {1}: (13, {}), {2}: (14, {}), {3}: (15, {})} | custom-call | flops 1048576000 | bytes 20971520 | tf_op jit(solution)/shard_map/mixer/pallas_call | solution.py:205
  198.4 18.4 %mixer.6 = (bf16[128,8192]{1,0:T(8,128)(2,1)}, bf16[128,8192]{1,0:T(8,128)(2,1)}, bf16[128,8192]{1,0:T(8,128)(2,1)}, bf16[128,8192]{1,0:T(8,128)(2,1)}, f32[4,8,...) custom-call(bf16[128,8192]{1,0:T(8,128)(2,1)} %bitcast.72, ...), custom_call_target="tpu_custom_call", output_to_operand_aliasing={{0}: (12, {}), {1}: (13, {}), {2}: (14, {}), {3}: (15, {})} | custom-call | flops 1048576000 | bytes 20971520 | tf_op jit(solution)/shard_map/mixer/pallas_call | solution.py:205
  216.9 18.4 %mixer.7 = (bf16[128,8192]{1,0:T(8,128)(2,1)}, bf16[128,8192]{1,0:T(8,128)(2,1)}, bf16[128,8192]{1,0:T(8,128)(2,1)}, bf16[128,8192]{1,0:T(8,128)(2,1)}, f32[4,8,...) custom-call(bf16[128,8192]{1,0:T(8,128)(2,1)} %bitcast.73, ...), custom_call_target="tpu_custom_call", output_to_operand_aliasing={{0}: (12, {}), {1}: (13, {}), {2}: (14, {}), {3}: (15, {})} | custom-call | flops 1048576000 | bytes 20971520 | tf_op jit(solution)/shard_map/mixer/pallas_call | solution.py:205
  237.3 26.5 %reduce-scatter.21.cloned.1.call-done = f32[1,8,40,256]{3,2,1,0:T(8,128)} async-done(((f32[4,8,40,256]{3,2,1,0:T(8,128)}), f32[1,8,40,256]{3,2,1,0:T(8,128)}) %reduce-scatter.21.cloned.1.call-update) | async-done | bytes 327696 | tf_op jit(solution)/shard_map/reduce_scatter | solution.py:226
  263.9 29.2 %reduce-scatter.17.cloned.1.call-done = f32[1,8,40,256]{3,2,1,0:T(8,128)} async-done(((f32[4,8,40,256]{3,2,1,0:T(8,128)}), f32[1,8,40,256]{3,2,1,0:T(8,128)}) %reduce-scatter.17.cloned.1.call-update) | async-done | bytes 327696 | tf_op jit(solution)/shard_map/reduce_scatter | solution.py:226
  306.2 15.8 %reduce-scatter.13.cloned.1.call-done = f32[1,8,40,256]{3,2,1,0:T(8,128)} async-done(((f32[4,8,40,256]{3,2,1,0:T(8,128)}), f32[1,8,40,256]{3,2,1,0:T(8,128)}) %reduce-scatter.13.cloned.1.call-update) | async-done | bytes 327696 | tf_op jit(solution)/shard_map/reduce_scatter | solution.py:226
  322.9 28.4 %reduce-scatter.9.cloned.1.call-done = f32[1,8,40,256]{3,2,1,0:T(8,128)} async-done(((f32[4,8,40,256]{3,2,1,0:T(8,128)}), f32[1,8,40,256]{3,2,1,0:T(8,128)}) %reduce-scatter.9.cloned.1.call-update) | async-done | bytes 327696 | tf_op jit(solution)/shard_map/reduce_scatter | solution.py:226
  351.9 63.8 %reduce-scatter.23.cloned.1.call-done = f32[1,40,256]{2,1,0:T(8,128)} async-done(((f32[8,40,256]{2,1,0:T(8,128)}), f32[1,40,256]{2,1,0:T(8,128)}) %reduce-scatter.23.cloned.1.call-update) | async-done | bytes 40976 | tf_op jit(solution)/shard_map/reduce_scatter | solution.py:227
  415.7 63.6 %reduce-scatter.19.cloned.1.call-done = f32[1,40,256]{2,1,0:T(8,128)} async-done(((f32[8,40,256]{2,1,0:T(8,128)}), f32[1,40,256]{2,1,0:T(8,128)}) %reduce-scatter.19.cloned.1.call-update) | async-done | bytes 40976 | tf_op jit(solution)/shard_map/reduce_scatter | solution.py:227
  479.4 63.6 %reduce-scatter.15.cloned.1.call-done = f32[1,40,256]{2,1,0:T(8,128)} async-done(((f32[8,40,256]{2,1,0:T(8,128)}), f32[1,40,256]{2,1,0:T(8,128)}) %reduce-scatter.15.cloned.1.call-update) | async-done | bytes 40976 | tf_op jit(solution)/shard_map/reduce_scatter | solution.py:227
  543.0 63.6 %reduce-scatter.11.cloned.1.call-done = f32[1,40,256]{2,1,0:T(8,128)} async-done(((f32[8,40,256]{2,1,0:T(8,128)}), f32[1,40,256]{2,1,0:T(8,128)}) %reduce-scatter.11.cloned.1.call-update) | async-done | bytes 40976 | tf_op jit(solution)/shard_map/reduce_scatter | solution.py:227
  608.2 5.4 all_gather.27
  (122 shorter events, 39.6 us)
Async XLA Ops:
  7.2 152.2 %all-gather.5.cloned.1.call-start = ((), (), s32[]{:S(2)}) async-start(), calls=%async_computation.16 | async-start | bytes 2621440 | tf_op jit(solution)/shard_map/all_gather | solution.py:155
  43.5 220.3 %reduce-scatter.21.cloned.1.call-start = ((), (), s32[]{:S(2)}) async-start(), calls=%async_computation.14 | async-start | bytes 1638400 | tf_op jit(solution)/shard_map/reduce_scatter | solution.py:226
  43.7 39.2 %collective-permute-start.9 = (bf16[3,8,2048]{2,1,0:T(8,128)(2,1)S(1)}, bf16[3,8,2048]{2,1,0:T(8,128)(2,1)S(1)}, u32[]{:S(2)}, u32[]{:S(2)}) collective-permute-start(bf16[3,8,2048]{2,1,0:T(8,128)(2,1)S(1)} %bitcast.132), channel_id=1, source_target_pairs={{0,1},{1,2},{2,3},{3,4},{4,5},{5,6},{6,7},{8,9},{9,10},{10,11},{11... | collective-permute-start | bytes 294920 | tf_op jit(solution)/shard_map/ppermute | solution.py:160
  47.2 47.3 %collective-permute-start.6 = (bf16[3,8,2048]{2,1,0:T(8,128)(2,1)S(1)}, bf16[3,8,2048]{2,1,0:T(8,128)(2,1)S(1)}, u32[]{:S(2)}, u32[]{:S(2)}) collective-permute-start(bf16[3,8,2048]{2,1,0:T(8,128)(2,1)S(1)} %bitcast.129), channel_id=1, source_target_pairs={{0,1},{1,2},{2,3},{3,4},{4,5},{5,6},{6,7},{8,9},{9,10},{10,11},{11... | collective-permute-start | bytes 294920 | tf_op jit(solution)/shard_map/ppermute | solution.py:160
  90.4 53.7 %collective-permute-start.10 = (bf16[128,2048]{1,0:T(8,128)(2,1)}, bf16[128,2048]{1,0:T(8,128)(2,1)S(1)}, u32[]{:S(2)}, u32[]{:S(2)}) collective-permute-start(bf16[128,2048]{1,0:T(8,128)(2,1)} %get-tuple-element.48.refs_6_), channel_id=1, source_target_pairs={{0,1},{1,2},{2,3},{3,4},{4,5},{5,6},{6,7},{8,9},{9,10},{10,11},{11... | collective-permute-start | bytes 1572872 | tf_op jit(solution)/shard_map/ppermute | solution.py:188
  93.2 59.3 %collective-permute-start.11 = (bf16[128,2048]{1,0:T(8,128)(2,1)}, bf16[128,2048]{1,0:T(8,128)(2,1)S(1)}, u32[]{:S(2)}, u32[]{:S(2)}) collective-permute-start(bf16[128,2048]{1,0:T(8,128)(2,1)} %get-tuple-element.49.refs_8_), channel_id=1, source_target_pairs={{1,0},{2,1},{3,2},{4,3},{5,4},{6,5},{7,6},{9,8},{10,9},{11,10},{12... | collective-permute-start | bytes 1572872 | tf_op jit(solution)/shard_map/ppermute | solution.py:188
  102.0 55.9 %collective-permute-start.7 = (bf16[128,2048]{1,0:T(8,128)(2,1)}, bf16[128,2048]{1,0:T(8,128)(2,1)}, u32[]{:S(2)}, u32[]{:S(2)}) collective-permute-start(bf16[128,2048]{1,0:T(8,128)(2,1)} %get-tuple-element.46.refs_6_), channel_id=1, source_target_pairs={{0,1},{1,2},{2,3},{3,4},{4,5},{5,6},{6,7},{8,9},{9,10},{10,11},{11... | collective-permute-start | bytes 1572872 | tf_op jit(solution)/shard_map/ppermute | solution.py:188
  107.4 22.7 %collective-permute-start.3 = (bf16[3,8,2048]{2,1,0:T(8,128)(2,1)S(1)}, bf16[3,8,2048]{2,1,0:T(8,128)(2,1)S(1)}, u32[]{:S(2)}, u32[]{:S(2)}) collective-permute-start(bf16[3,8,2048]{2,1,0:T(8,128)(2,1)S(1)} %bitcast.126), channel_id=1, source_target_pairs={{0,1},{1,2},{2,3},{3,4},{4,5},{5,6},{6,7},{8,9},{9,10},{10,11},{11... | collective-permute-start | bytes 294920 | tf_op jit(solution)/shard_map/ppermute | solution.py:160
  109.4 70.4 %collective-permute-start.8 = (bf16[128,2048]{1,0:T(8,128)(2,1)}, bf16[128,2048]{1,0:T(8,128)(2,1)}, u32[]{:S(2)}, u32[]{:S(2)}) collective-permute-start(bf16[128,2048]{1,0:T(8,128)(2,1)} %get-tuple-element.47.refs_8_), channel_id=1, source_target_pairs={{1,0},{2,1},{3,2},{4,3},{5,4},{6,5},{7,6},{9,8},{10,9},{11,10},{12... | collective-permute-start | bytes 1572872 | tf_op jit(solution)/shard_map/ppermute | solution.py:188
  130.1 11.3 %collective-permute-start = (bf16[3,8,2048]{2,1,0:T(8,128)(2,1)S(1)}, bf16[3,8,2048]{2,1,0:T(8,128)(2,1)S(1)}, u32[]{:S(2)}, u32[]{:S(2)}) collective-permute-start(bf16[3,8,2048]{2,1,0:T(8,128)(2,1)S(1)} %bitcast.125), channel_id=1, source_target_pairs={{0,1},{1,2},{2,3},{3,4},{4,5},{5,6},{6,7},{8,9},{9,10},{10,11},{11... | collective-permute-start | bytes 294920 | tf_op jit(solution)/shard_map/ppermute | solution.py:160
  141.4 56.9 %collective-permute-start.4 = (bf16[128,2048]{1,0:T(8,128)(2,1)}, bf16[128,2048]{1,0:T(8,128)(2,1)}, u32[]{:S(2)}, u32[]{:S(2)}) collective-permute-start(bf16[128,2048]{1,0:T(8,128)(2,1)} %get-tuple-element.44.refs_6_), channel_id=1, source_target_pairs={{0,1},{1,2},{2,3},{3,4},{4,5},{5,6},{6,7},{8,9},{9,10},{10,11},{11... | collective-permute-start | bytes 1572872 | tf_op jit(solution)/shard_map/ppermute | solution.py:188
  144.2 54.2 %collective-permute-start.5 = (bf16[128,2048]{1,0:T(8,128)(2,1)}, bf16[128,2048]{1,0:T(8,128)(2,1)}, u32[]{:S(2)}, u32[]{:S(2)}) collective-permute-start(bf16[128,2048]{1,0:T(8,128)(2,1)} %get-tuple-element.45.refs_8_), channel_id=1, source_target_pairs={{1,0},{2,1},{3,2},{4,3},{5,4},{6,5},{7,6},{9,8},{10,9},{11,10},{12... | collective-permute-start | bytes 1572872 | tf_op jit(solution)/shard_map/ppermute | solution.py:188
  153.3 63.5 %collective-permute-start.1 = (bf16[128,2048]{1,0:T(8,128)(2,1)}, bf16[128,2048]{1,0:T(8,128)(2,1)S(1)}, u32[]{:S(2)}, u32[]{:S(2)}) collective-permute-start(bf16[128,2048]{1,0:T(8,128)(2,1)} %get-tuple-element.42.refs_6_), channel_id=1, source_target_pairs={{0,1},{1,2},{2,3},{3,4},{4,5},{5,6},{6,7},{8,9},{9,10},{10,11},{11... | collective-permute-start | bytes 1572872 | tf_op jit(solution)/shard_map/ppermute | solution.py:188
  157.9 59.0 %collective-permute-start.2 = (bf16[128,2048]{1,0:T(8,128)(2,1)}, bf16[128,2048]{1,0:T(8,128)(2,1)}, u32[]{:S(2)}, u32[]{:S(2)}) collective-permute-start(bf16[128,2048]{1,0:T(8,128)(2,1)} %get-tuple-element.43.refs_8_), channel_id=1, source_target_pairs={{1,0},{2,1},{3,2},{4,3},{5,4},{6,5},{7,6},{9,8},{10,9},{11,10},{12... | collective-permute-start | bytes 1572872 | tf_op jit(solution)/shard_map/ppermute | solution.py:188
  235.3 57.8 %reduce-scatter.17.cloned.1.call-start = ((), (), s32[]{:S(2)}) async-start(), calls=%async_computation.12 | async-start | bytes 1638400 | tf_op jit(solution)/shard_map/reduce_scatter | solution.py:226
  236.1 86.0 %reduce-scatter.13.cloned.1.call-start = ((), (), s32[]{:S(2)}) async-start(), calls=%async_computation.10 | async-start | bytes 1638400 | tf_op jit(solution)/shard_map/reduce_scatter | solution.py:226
  236.6 114.6 %reduce-scatter.9.cloned.1.call-start = ((), (), s32[]{:S(2)}) async-start(), calls=%async_computation.8 | async-start | bytes 1638400 | tf_op jit(solution)/shard_map/reduce_scatter | solution.py:226
  237.2 178.5 %reduce-scatter.23.cloned.1.call-start = ((), (), s32[]{:S(2)}) async-start(), calls=%async_computation.15 | async-start | bytes 368640 | tf_op jit(solution)/shard_map/reduce_scatter | solution.py:227
  263.8 215.5 %reduce-scatter.19.cloned.1.call-start = ((), (), s32[]{:S(2)}) async-start(), calls=%async_computation.13 | async-start | bytes 368640 | tf_op jit(solution)/shard_map/reduce_scatter | solution.py:227
  293.1 249.8 %reduce-scatter.15.cloned.1.call-start = ((), (), s32[]{:S(2)}) async-start(), calls=%async_computation.11 | async-start | bytes 368640 | tf_op jit(solution)/shard_map/reduce_scatter | solution.py:227
  294.5 7.8 %collective-permute-start.14 = (bf16[3,8,2048]{2,1,0:T(8,128)(2,1)S(1)}, bf16[3,8,2048]{2,1,0:T(8,128)(2,1)S(1)}, u32[]{:S(2)}, u32[]{:S(2)}) collective-permute-start(bf16[3,8,2048]{2,1,0:T(8,128)(2,1)S(1)} %copy-done.25), channel_id=1, source_target_pairs={{1,0},{2,1},{3,2},{4,3},{5,4},{6,5},{7,6},{9,8},{10,9},{11,10},{12... | collective-permute-start | bytes 294920 | tf_op jit(solution)/shard_map/ppermute | solution.py:228
  295.8 8.8 %collective-permute-start.13 = (bf16[3,8,2048]{2,1,0:T(8,128)(2,1)S(1)}, bf16[3,8,2048]{2,1,0:T(8,128)(2,1)S(1)}, u32[]{:S(2)}, u32[]{:S(2)}) collective-permute-start(bf16[3,8,2048]{2,1,0:T(8,128)(2,1)S(1)} %get-tuple-element.69), channel_id=1, source_target_pairs={{1,0},{2,1},{3,2},{4,3},{5,4},{6,5},{7,6},{9,8},{10,9},{11,10},{12... | collective-permute-start | bytes 294920 | tf_op jit(solution)/shard_map/ppermute | solution.py:228
  297.1 8.9 %collective-permute-start.12 = (bf16[3,8,2048]{2,1,0:T(8,128)(2,1)S(1)}, bf16[3,8,2048]{2,1,0:T(8,128)(2,1)S(1)}, u32[]{:S(2)}, u32[]{:S(2)}) collective-permute-start(bf16[3,8,2048]{2,1,0:T(8,128)(2,1)S(1)} %copy-done.23), channel_id=1, source_target_pairs={{1,0},{2,1},{3,2},{4,3},{5,4},{6,5},{7,6},{9,8},{10,9},{11,10},{12... | collective-permute-start | bytes 294920 | tf_op jit(solution)/shard_map/ppermute | solution.py:228
  322.1 284.5 %reduce-scatter.11.cloned.1.call-start = ((), (), s32[]{:S(2)}) async-start(), calls=%async_computation.9 | async-start | bytes 368640 | tf_op jit(solution)/shard_map/reduce_scatter | solution.py:227
  (31 other events, 643.5 us)
Sparse Core Ops, SparseCore 0:
  43.7 23.6 all-gather.4
  235.5 28.3 reduce-scatter.20
  266.5 26.5 reduce-scatter.16
  295.5 26.5 reduce-scatter.12
  324.6 26.5 reduce-scatter.8
  354.3 61.3 reduce-scatter.22
  419.0 60.3 reduce-scatter.18
  482.6 60.2 reduce-scatter.14
  546.2 60.2 reduce-scatter.10

commit v2 on v1

--- a/solution.py
+++ b/solution.py
@@ -49,13 +49,50 @@
     return total
 
 
+def bits_of(count):
+    return [b for b in range(count.bit_length() - 1)]
+
+
+def swap(x, axis, count, bit):
+    return lax.ppermute(x, axis, [(i, i ^ (1 << bit)) for i in range(count)])
+
+
+def gather(block, axis, count):
+    me = lax.axis_index(axis)
+    rest = block.shape
+    zeros = (0,) * len(rest)
+    held = lax.dynamic_update_slice(jnp.zeros((count,) + rest, block.dtype), block[None], (me,) + zeros)
+    for bit in reversed(bits_of(count)):
+        low = 1 << bit
+        view = held.reshape((count // (2 * low), 2, low) + rest)
+        mine = (me // low) % 2
+        own = lax.dynamic_slice(view, (0, mine, me % low) + zeros, (count // (2 * low), 1, 1) + rest)
+        other = swap(own, axis, count, bit)
+        view = lax.dynamic_update_slice(view, other, (0, 1 - mine, me % low) + zeros)
+        held = view.reshape((count,) + rest)
+    return held
+
+
+def scatter_sum(x, axis, count, narrow):
+    me = lax.axis_index(axis)
+    for bit in bits_of(count):
+        mine = (me >> bit) % 2
+        view = x.reshape((x.shape[0] // 2, 2) + x.shape[1:])
+        send = lax.dynamic_index_in_dim(view, 1 - mine, 1, keepdims=False)
+        keep = lax.dynamic_index_in_dim(view, mine, 1, keepdims=False)
+        if bit in narrow:
+            send = send.astype(BF)
+        x = keep + swap(send, axis, count, bit).astype(F32)
+    return x[0]
+
+
 def first_kernel(width, q_ref, k_ref, v_ref, g_ref, halo_ref, s_ref, u_ref, d_ref, pad_ref):
     count = q_ref.shape[0]
 
     def conv(i, ref):
         pad_ref[0:HALO] = halo_ref[i].astype(F32)
         pad_ref[HALO:] = ref[...].astype(F32)
-        return short_conv(pad_ref, s_ref[i], width, count)
+        return short_conv(pad_ref, s_ref[i // s_ref.shape[1], i % s_ref.shape[1]], width, count)
 
     ks = conv(1, k_ref)
     u_ref[...] = (ks * conv(2, v_ref)).astype(BF)
@@ -69,6 +106,9 @@
     length = q_ref.shape[0]
     chans = q_ref.shape[1]
 
+    def taps_of(i):
+        return s_ref[i // s_ref.shape[1], i % s_ref.shape[1]]
+
     def double(x):
         return jnp.concatenate([x, x], axis=0)
 
@@ -102,14 +142,14 @@
     def load(i, ref, pad):
         pad[0:HALO] = halo_ref[i].astype(F32)
         pad[HALO:] = ref[...].astype(F32)
-        return short_conv(pad, s_ref[i], width, length)
+        return short_conv(pad, taps_of(i), width, length)
 
     padg[0:HALO] = jnp.zeros((HALO, chans), F32)
     padg[HALO + length :] = jnp.zeros((HALO, chans), F32)
 
     def finish(i, grads, pad, out_ref):
         padg[HALO : HALO + length] = grads
-        taps = s_ref[i]
+        taps = taps_of(i)
         total = taps[0:1] * grads
         head = taps[1:2] * padg[1 : 1 + HALO]
         sums = [jnp.sum(grads * pad[HALO : HALO + length], axis=0, keepdims=True)]
@@ -144,20 +184,21 @@
     part = chans // pieces
     cb = 256 if part % 256 == 0 else 128
     inner = part // cb
-    slot = HALO * (-(-3 // n_dp))
+    per = -(-3 // n_dp)
+    slot = HALO * per
     right = [(i, i + 1) for i in range(n_ctx - 1)]
     left = [(i + 1, i) for i in range(n_ctx - 1)]
     assert n_dp * share == length and width - 1 <= HALO
 
-    shorts = jnp.pad(short_filter.transpose(0, 2, 1), ((0, 0), (0, HALO - width), (0, 0)))
-    shorts = lax.all_gather(shorts, "context")
-    taps = lax.all_gather(med_filter.astype(BF).T, "context")
-    taps = lax.all_gather(taps, "dp")
+    shorts = jnp.pad(short_filter.transpose(0, 2, 1), ((0, n_dp * per - 3), (0, HALO - width), (0, 0)))
+    shorts = lax.dynamic_slice_in_dim(shorts, lax.axis_index("dp") * per, per, 0)
+    shorts = gather(gather(shorts, "context", n_ctx), "dp", n_dp)
+    taps, shorts = lax.optimization_barrier((med_filter.astype(BF).T, shorts))
+    taps = gather(gather(taps, "context", n_ctx), "dp", n_dp)
     table = jnp.asarray(tables(length))
 
     rim = jnp.stack([a[length - HALO :] for a in (q, k, v)])
-    rim = rim.reshape(3, HALO, n_ctx, pieces, part)
-    rims = [lax.ppermute(rim[:, :, :, c].reshape(3, HALO, n_ctx * part), "context", right) for c in range(pieces)]
+    rims = lax.ppermute(rim, "context", right)
 
     def whole(c):
         return pl.BlockSpec((length, cb), lambda b, i: (0, b * (chans // cb) + c * inner + i))
@@ -165,8 +206,11 @@
     piece = pl.BlockSpec((length, cb), lambda b, i: (0, b * inner + i))
     rim_spec = pl.BlockSpec((3, HALO, cb), lambda b, i: (0, 0, b * inner + i))
 
+    def edge(c):
+        return pl.BlockSpec((3, HALO, cb), lambda b, i: (0, 0, b * (chans // cb) + c * inner + i))
+
     def short_spec(c):
-        return pl.BlockSpec((pl.squeezed, 3, HALO, cb), lambda b, i: (b, 0, 0, c * inner + i))
+        return pl.BlockSpec((n_dp, pl.squeezed, per, HALO, cb), lambda b, i: (0, b, 0, 0, c * inner + i))
 
     sent = []
     for c in range(pieces):
@@ -174,7 +218,7 @@
             pl.pallas_call(
                 functools.partial(first_kernel, width),
                 grid=(n_ctx, inner),
-                in_specs=[whole(c)] * 4 + [rim_spec, short_spec(c)],
+                in_specs=[whole(c)] * 4 + [edge(c), short_spec(c)],
                 out_specs=[piece] * 2,
                 out_shape=[jax.ShapeDtypeStruct((length, n_ctx * part), BF)] * 2,
                 scratch_shapes=[pltpu.VMEM((HALO + length, cb), F32)],
@@ -182,7 +226,7 @@
                     flops=50 * length * n_ctx * part, bytes_accessed=24 * length * n_ctx * part, transcendentals=0
                 ),
                 name="featurize",
-            )(q, k, v, g, rims[c], shorts)
+            )(q, k, v, g, rims, shorts)
         )
     arrived = [
         (lax.ppermute(u, "context", right), lax.ppermute(d, "context", left)) for u, d in sent
@@ -195,8 +239,8 @@
     for c in range(pieces):
         tap_spec = pl.BlockSpec((n_dp, 1, share, cb), lambda b, i, c=c: (0, b, 0, c * inner + i))
         table_spec = pl.BlockSpec(table.shape, lambda b, i: (0, 0, 0))
-        args = [q, k, v, g, rims[c], shorts, sent[c][0], arrived[c][0], sent[c][1], arrived[c][1], taps, table]
-        specs = [whole(c)] * 4 + [rim_spec, short_spec(c)] + [piece] * 4 + [tap_spec, table_spec]
+        args = [q, k, v, g, rims, shorts, sent[c][0], arrived[c][0], sent[c][1], arrived[c][1], taps, table]
+        specs = [whole(c)] * 4 + [edge(c), short_spec(c)] + [piece] * 4 + [tap_spec, table_spec]
         alias = {}
         if grown is not None:
             alias = {len(args) + i: i for i in range(4)}
@@ -223,10 +267,20 @@
             name="mixer",
         )(*args)
         grown = list(outs[:4])
-        total = lax.psum_scatter(outs[4], "dp", scatter_dimension=0)
-        sums.append(lax.psum_scatter(total, "context", scatter_dimension=0))
-        heads.append(lax.ppermute(outs[5], "context", left))
+        sums.append(outs[4])
+        heads.append(outs[5])
         tails.append(outs[6])
+
+    def reduce(items):
+        x = jnp.concatenate(items, axis=3) if len(items) > 1 else items[0]
+        x = scatter_sum(x, "dp", n_dp, (1,))
+        return scatter_sum(x, "context", n_ctx, (0,))
+
+    groups = [(0, pieces - 1), (pieces - 1, pieces)] if pieces > 1 else [(0, 1)]
+    sums = [reduce(sums[a:b]) for a, b in groups]
+    heads = [
+        h for a, b in groups for h in jnp.split(lax.ppermute(jnp.concatenate(heads[a:b], axis=0), "context", left), b - a)
+    ]
 
     def join(items):
         return jnp.concatenate([a.reshape(3, HALO, n_ctx, 1, part) for a in items], axis=3).reshape(3, HALO, full)
@@ -235,7 +289,7 @@
     grads = [lax.dynamic_update_slice(a, fixed[i], (length - HALO, 0)) for i, a in enumerate(grown[1:])]
     total = jnp.concatenate(sums, axis=1)
     grad_med = total[:share].T
-    short = lax.all_gather(total[share:], "dp", tiled=True)[: 3 * HALO]
+    short = gather(total[share:], "dp", n_dp).reshape(-1, chans)[: 3 * HALO]
     grad_short = short.reshape(3, HALO, chans)[:, :width].transpose(0, 2, 1)
     return (grown[0][None], grads[0][None], grads[1][None], grads[2][None], grad_med, grad_short)
 

time: 624 us -> 308 us (0.49)
  waiting for transfers between devices: 384 us -> 108 us
  blocking collectives: 74.4 us -> 0 us
  starting transfers between devices: 38.2 us -> 69.8 us
  local copies, waits for them, and re-layouts: 6.92 us -> 20.6 us
  between operations: 14.4 us -> 1.5 us
    reduce_scatter x8 -> x0, waiting for transfers between devices: 355 us -> none  [the longest x4 255 us: per_device(): sums.append(lax.psum_scatter(total, 'context', scatter_dimension=0))]
    all_gather x3 -> x0, blocking collectives: 74.4 us -> none  [the longest x1 35.2 us: per_device(): taps = lax.all_gather(med_filter.astype(BF).T, 'context')]
    ppermute x8 -> x25, waiting for transfers between devices: 27.1 us -> 70 us  [the longest x22 55.7 us: swap(): return lax.ppermute(x, axis, [(i, i ^ 1 << bit) for i in range(count)])]
    ppermute x4, waiting for transfers between devices: 0.01 us -> 37.7 us  [per_device(): lax.ppermute(u, 'context', right)]
    ppermute x8 -> x25, starting transfers between devices: 17 us -> 44.1 us  [the longest x22 38.1 us: swap(): return lax.ppermute(x, axis, [(i, i ^ 1 << bit) for i in range(count)])]
    unnamed x54 -> x52, local copies, waits for them, and re-layouts: 4.09 us -> 10.5 us
  transfers between devices with their start and end apart: 25 -> 33, of which waited for: 13 -> 20; matrix products, arithmetic and copies ran while one was open for 0% -> 3% of each run, Pallas kernels for 13% -> 27%
where the time goes in v2:
time: 308 us; the launch traced here: 306 us
  waiting for transfers between devices  108 us (35%)
  Pallas kernels  101 us (33%)
  starting transfers between devices  69.8 us (23%)
  local copies, waits for them, and re-layouts  20.6 us (7%)
  other arithmetic  5.07 us (2%)
    pallas_call x4, Pallas kernels, per_device(): pl.pallas_call(functools.partial(second_kernel, width), grid=(n_ctx, inne...  73.7 us
    ppermute x22, waiting for transfers between devices, swap(): return lax.ppermute(x, axis, [(i, i ^ 1 << bit) for i in range(count)])  55.7 us
    ppermute x22, starting transfers between devices, swap(): return lax.ppermute(x, axis, [(i, i ^ 1 << bit) for i in range(count)])  38.1 us
    ppermute x4, waiting for transfers between devices, per_device(): lax.ppermute(u, 'context', right)  37.7 us
    pallas_call x4, Pallas kernels, per_device(): pl.pallas_call(functools.partial(first_kernel, width), grid=(n_ctx, inner...  27.6 us
    ppermute x4, starting transfers between devices, per_device(): lax.ppermute(u, 'context', right)  20.5 us
    unnamed x52, local copies, waits for them, and re-layouts  10.5 us
    ppermute x1, waiting for transfers between devices, per_device(): rims = lax.ppermute(rim, 'context', right)  8.99 us
  transfers between devices with their start and end apart: 33, of which 20 were waited for; matrix products, arithmetic and copies ran while one was open for 3% of the time, Pallas kernels for 27%

profile of v2, /device:TPU:0, one launch (start us, length us, event | category | flops | bytes accessed | tf_op | source)
XLA Modules:
  0.0 306.0 jit_solution(1888468288797200257)
XLA Ops:
  1.5 4.1 %collective-permute-start.1 = (f32[1,1,1,1,8,1024]{5,4,2,1,3,0:T(8,128)S(1)}, f32[1,1,1,1,8,1024]{5,4,2,1,3,0:T(8,128)S(1)}, u32[]{:S(2)}, u32[]{:S(2)}) collective-permute-start(f32[1,1,1,1,8,1024]{5,4,2,1,3,0:T(8,128)S(1)} %constant_dynamic-slice_fusion.13), channel_id=1, source_target_pairs={{0,4},{1,5},{2,6},{3,7},{4,0},{5,1},{6,2},{7,3},{8,12},{9,13},{10,... | collective-permute-start | bytes 98312 | tf_op jit(solution)/shard_map/ppermute | solution.py:57
  19.0 4.9 %collective-permute-done.4 = f32[1,1,1,8,1,8,1024]{6,5,3,2,1,4,0:T(8,128)S(1)} collective-permute-done((f32[1,1,1,8,1,8,1024]{6,5,3,2,1,4,0:T(8,128)S(1)}, f32[1,1,1,8,1,8,1024]{6,5,3,2,1,4,0:T(8,128)S(1)}, u32[]{:S(2)}, u32[]{:S(2)}) %collective-permute-start.4) | collective-permute-done | bytes 262176 | tf_op jit(solution)/shard_map/ppermute | solution.py:57
  28.8 4.0 %collective-permute-done.8 = bf16[1,1,1,32,1024]{4,3,2,1,0:T(8,128)(2,1)S(1)} collective-permute-done((bf16[1,1,1,32,1024]{4,3,2,1,0:T(8,128)(2,1)S(1)}, bf16[1,1,1,32,1024]{4,3,2,1,0:T(8,128)(2,1)S(1)}, u32[]{:S(2)}, u32[]{:S(2)}) %collective-permute-start.8) | collective-permute-done | bytes 65568 | tf_op jit(solution)/shard_map/ppermute | solution.py:57
  33.4 4.4 %collective-permute-done.9 = bf16[2,1,1,32,1024]{4,3,2,1,0:T(8,128)(2,1)S(1)} collective-permute-done((bf16[2,1,1,32,1024]{4,3,2,1,0:T(8,128)(2,1)S(1)}, bf16[2,1,1,32,1024]{4,3,2,1,0:T(8,128)(2,1)S(1)}, u32[]{:S(2)}, u32[]{:S(2)}) %collective-permute-start.9) | collective-permute-done | bytes 131104 | tf_op jit(solution)/shard_map/ppermute | solution.py:57
  39.7 4.7 %collective-permute-done.10 = bf16[4,1,1,32,1024]{4,3,1,0,2:T(8,128)(2,1)S(1)} collective-permute-done((bf16[4,1,1,32,1024]{4,3,1,0,2:T(8,128)(2,1)S(1)}, bf16[4,1,1,32,1024]{4,3,1,0,2:T(8,128)(2,1)S(1)}, u32[]{:S(2)}, u32[]{:S(2)}) %collective-permute-start.10) | collective-permute-done | bytes 262176 | tf_op jit(solution)/shard_map/ppermute | solution.py:57
  46.3 8.8 %collective-permute-done.11 = bf16[1,1,1,8,32,1024]{5,4,3,2,1,0:T(8,128)(2,1)S(1)} collective-permute-done((bf16[1,1,1,8,32,1024]{5,4,3,2,1,0:T(8,128)(2,1)S(1)}, bf16[1,1,1,8,32,1024]{5,4,3,2,1,0:T(8,128)(2,1)S(1)}, u32[]{:S(2)}, u32[]{:S(2)}) %collective-permute-start.11) | collective-permute-done | bytes 524320 | tf_op jit(solution)/shard_map/ppermute | solution.py:57
  59.9 9.0 %collective-permute-done.halo_ref.refs_4_ = bf16[3,8,8192]{2,1,0:T(8,128)(2,1)S(1)} collective-permute-done((bf16[3,8,8192]{2,1,0:T(8,128)(2,1)S(1)}, bf16[3,8,8192]{2,1,0:T(8,128)(2,1)S(1)}, u32[]{:S(2)}, u32[]{:S(2)}) %collective-permute-start) | collective-permute-done | bytes 393248 | tf_op jit(solution)/shard_map/ppermute | solution.py:201
  69.7 6.8 %featurize.7 = (bf16[128,2048]{1,0:T(8,128)(2,1)}, bf16[128,2048]{1,0:T(8,128)(2,1)}) custom-call(bf16[128,8192]{1,0:T(8,128)(2,1)} %bitcast.111, bf16[128,8192]{1,0:T(8,128)(2,1)} %bitcast.119, bf16[128,8192]{1,0:T(8,128)(2,1)} %bitcast.127, bf16[128,8192]{1,0:T(8,128)(2,1)} %bitcast.135, bf16[3,8,8192]{2,1,0:T(8,128)(2,1)} %copy-done.3, ...), custom_call_target="tpu_custom_call" | custom-call | flops 13107200 | bytes 6291456 | tf_op jit(solution)/shard_map/featurize/pallas_call | solution.py:218
  76.5 5.6 %collective-permute-start.17 = (bf16[128,2048]{1,0:T(8,128)(2,1)}, bf16[128,2048]{1,0:T(8,128)(2,1)S(1)}, u32[]{:S(2)}, u32[]{:S(2)}) collective-permute-start(bf16[128,2048]{1,0:T(8,128)(2,1)} %get-tuple-element.52.refs_6_), channel_id=1, source_target_pairs={{0,1},{1,2},{2,3},{3,4},{4,5},{5,6},{6,7},{8,9},{9,10},{10,11},{11... | collective-permute-start | bytes 1572872 | tf_op jit(solution)/shard_map/ppermute | solution.py:232
  83.3 6.9 %featurize.6 = (bf16[128,2048]{1,0:T(8,128)(2,1)}, bf16[128,2048]{1,0:T(8,128)(2,1)}) custom-call(bf16[128,8192]{1,0:T(8,128)(2,1)} %bitcast.112, bf16[128,8192]{1,0:T(8,128)(2,1)} %bitcast.120, bf16[128,8192]{1,0:T(8,128)(2,1)} %bitcast.128, bf16[128,8192]{1,0:T(8,128)(2,1)} %bitcast.136, bf16[3,8,8192]{2,1,0:T(8,128)(2,1)} %copy-done.3, ...), custom_call_target="tpu_custom_call" | custom-call | flops 13107200 | bytes 6291456 | tf_op jit(solution)/shard_map/featurize/pallas_call | solution.py:218
  90.2 5.9 %collective-permute-start.15 = (bf16[128,2048]{1,0:T(8,128)(2,1)}, bf16[128,2048]{1,0:T(8,128)(2,1)S(1)}, u32[]{:S(2)}, u32[]{:S(2)}) collective-permute-start(bf16[128,2048]{1,0:T(8,128)(2,1)} %get-tuple-element.50.refs_6_), channel_id=1, source_target_pairs={{0,1},{1,2},{2,3},{3,4},{4,5},{5,6},{6,7},{8,9},{9,10},{10,11},{11... | collective-permute-start | bytes 1572872 | tf_op jit(solution)/shard_map/ppermute | solution.py:232
  97.4 6.9 %featurize.5 = (bf16[128,2048]{1,0:T(8,128)(2,1)}, bf16[128,2048]{1,0:T(8,128)(2,1)}) custom-call(bf16[128,8192]{1,0:T(8,128)(2,1)} %bitcast.113, bf16[128,8192]{1,0:T(8,128)(2,1)} %bitcast.121, bf16[128,8192]{1,0:T(8,128)(2,1)} %bitcast.129, bf16[128,8192]{1,0:T(8,128)(2,1)} %bitcast.137, bf16[3,8,8192]{2,1,0:T(8,128)(2,1)} %copy-done.3, ...), custom_call_target="tpu_custom_call" | custom-call | flops 13107200 | bytes 6291456 | tf_op jit(solution)/shard_map/featurize/pallas_call | solution.py:218
  104.3 12.8 %collective-permute-done.17.refs_7_ = bf16[128,2048]{1,0:T(8,128)(2,1)S(1)} collective-permute-done((bf16[128,2048]{1,0:T(8,128)(2,1)}, bf16[128,2048]{1,0:T(8,128)(2,1)S(1)}, u32[]{:S(2)}, u32[]{:S(2)}) %collective-permute-start.17) | collective-permute-done | bytes 524320 | tf_op jit(solution)/shard_map/ppermute | solution.py:232
  117.9 4.3 %collective-permute-start.13 = (bf16[128,2048]{1,0:T(8,128)(2,1)}, bf16[128,2048]{1,0:T(8,128)(2,1)S(1)}, u32[]{:S(2)}, u32[]{:S(2)}) collective-permute-start(bf16[128,2048]{1,0:T(8,128)(2,1)} %get-tuple-element.48.refs_6_), channel_id=1, source_target_pairs={{0,1},{1,2},{2,3},{3,4},{4,5},{5,6},{6,7},{8,9},{9,10},{10,11},{11... | collective-permute-start | bytes 1572872 | tf_op jit(solution)/shard_map/ppermute | solution.py:232
  129.0 18.4 %mixer.4 = (bf16[128,8192]{1,0:T(8,128)(2,1)}, bf16[128,8192]{1,0:T(8,128)(2,1)}, bf16[128,8192]{1,0:T(8,128)(2,1)}, bf16[128,8192]{1,0:T(8,128)(2,1)}, f32[4,8,...) custom-call(bf16[128,8192]{1,0:T(8,128)(2,1)} %bitcast.114, ...), custom_call_target="tpu_custom_call" | custom-call | flops 1048576000 | bytes 20971520 | tf_op jit(solution)/shard_map/mixer/pallas_call | solution.py:249
  148.1 18.4 %mixer.5 = (bf16[128,8192]{1,0:T(8,128)(2,1)}, bf16[128,8192]{1,0:T(8,128)(2,1)}, bf16[128,8192]{1,0:T(8,128)(2,1)}, bf16[128,8192]{1,0:T(8,128)(2,1)}, f32[4,8,...) custom-call(bf16[128,8192]{1,0:T(8,128)(2,1)} %bitcast.115, ...), custom_call_target="tpu_custom_call", output_to_operand_aliasing={{0}: (12, {}), {1}: (13, {}), {2}: (14, {}), {3}: (15, {})} | custom-call | flops 1048576000 | bytes 20971520 | tf_op jit(solution)/shard_map/mixer/pallas_call | solution.py:249
  167.2 18.4 %mixer.6 = (bf16[128,8192]{1,0:T(8,128)(2,1)}, bf16[128,8192]{1,0:T(8,128)(2,1)}, bf16[128,8192]{1,0:T(8,128)(2,1)}, bf16[128,8192]{1,0:T(8,128)(2,1)}, f32[4,8,...) custom-call(bf16[128,8192]{1,0:T(8,128)(2,1)} %bitcast.116, ...), custom_call_target="tpu_custom_call", output_to_operand_aliasing={{0}: (12, {}), {1}: (13, {}), {2}: (14, {}), {3}: (15, {})} | custom-call | flops 1048576000 | bytes 20971520 | tf_op jit(solution)/shard_map/mixer/pallas_call | solution.py:249
  189.7 7.0 %featurize.4 = (bf16[128,2048]{1,0:T(8,128)(2,1)}, bf16[128,2048]{1,0:T(8,128)(2,1)}) custom-call(bf16[128,8192]{1,0:T(8,128)(2,1)} %bitcast.117, bf16[128,8192]{1,0:T(8,128)(2,1)} %bitcast.125, bf16[128,8192]{1,0:T(8,128)(2,1)} %bitcast.133, bf16[128,8192]{1,0:T(8,128)(2,1)} %bitcast.141, bf16[3,8,8192]{2,1,0:T(8,128)(2,1)} %copy-done.3, ...), custom_call_target="tpu_custom_call" | custom-call | flops 13107200 | bytes 6291456 | tf_op jit(solution)/shard_map/featurize/pallas_call | solution.py:218
  196.7 4.8 %collective-permute-start.6 = (bf16[128,2048]{1,0:T(8,128)(2,1)}, bf16[128,2048]{1,0:T(8,128)(2,1)S(1)}, u32[]{:S(2)}, u32[]{:S(2)}) collective-permute-start(bf16[128,2048]{1,0:T(8,128)(2,1)} %get-tuple-element.45.refs_6_), channel_id=1, source_target_pairs={{0,1},{1,2},{2,3},{3,4},{4,5},{5,6},{6,7},{8,9},{9,10},{10,11},{11... | collective-permute-start | bytes 1572872 | tf_op jit(solution)/shard_map/ppermute | solution.py:232
  205.9 24.9 %collective-permute-done.6.refs_7_ = bf16[128,2048]{1,0:T(8,128)(2,1)S(1)} collective-permute-done((bf16[128,2048]{1,0:T(8,128)(2,1)}, bf16[128,2048]{1,0:T(8,128)(2,1)S(1)}, u32[]{:S(2)}, u32[]{:S(2)}) %collective-permute-start.6) | collective-permute-done | bytes 524320 | tf_op jit(solution)/shard_map/ppermute | solution.py:232
  232.9 18.4 %mixer.7 = (bf16[128,8192]{1,0:T(8,128)(2,1)}, bf16[128,8192]{1,0:T(8,128)(2,1)}, bf16[128,8192]{1,0:T(8,128)(2,1)}, bf16[128,8192]{1,0:T(8,128)(2,1)}, f32[4,8,...) custom-call(bf16[128,8192]{1,0:T(8,128)(2,1)} %bitcast.118, ...), custom_call_target="tpu_custom_call", output_to_operand_aliasing={{0}: (12, {}), {1}: (13, {}), {2}: (14, {}), {3}: (15, {})} | custom-call | flops 1048576000 | bytes 20971520 | tf_op jit(solution)/shard_map/mixer/pallas_call | solution.py:249
  253.8 5.4 %collective-permute-done.20 = bf16[3,8,2048]{2,1,0:T(8,128)(2,1)S(1)} collective-permute-done((bf16[3,8,2048]{2,1,0:T(8,128)(2,1)S(1)}, bf16[3,8,2048]{2,1,0:T(8,128)(2,1)S(1)}, u32[]{:S(2)}, u32[]{:S(2)}) %collective-permute-start.20) | collective-permute-done | bytes 98336 | tf_op jit(solution)/shard_map/ppermute | solution.py:282
  268.3 8.0 %collective-permute-done.22 = bf16[1,8,40,768]{3,2,1,0:T(8,128)(2,1)S(1)} collective-permute-done((bf16[1,8,40,768]{3,2,1,0:T(8,128)(2,1)S(1)}, bf16[1,8,40,768]{3,2,1,0:T(8,128)(2,1)S(1)}, u32[]{:S(2)}, u32[]{:S(2)}) %collective-permute-start.22) | collective-permute-done | bytes 491552 | tf_op jit(solution)/shard_map/ppermute | solution.py:57
  291.9 4.6 %collective-permute-start.25 = (f32[1,40,768]{2,1,0:T(8,128)S(1)}, f32[1,40,768]{2,1,0:T(8,128)S(1)}, u32[]{:S(2)}, u32[]{:S(2)}) collective-permute-start(f32[1,40,768]{2,1,0:T(8,128)S(1)} %constant_dynamic-slice_fusion.3), channel_id=1, source_target_pairs={{0,4},{1,5},{2,6},{3,7},{4,0},{5,1},{6,2},{7,3},{8,12},{9,13},{10,... | collective-permute-start | bytes 368648 | tf_op jit(solution)/shard_map/ppermute | solution.py:57
  (177 shorter events, 87.1 us)
Async XLA Ops:
  17.5 6.4 %collective-permute-start.4 = (f32[1,1,1,8,1,8,1024]{6,5,3,2,1,4,0:T(8,128)S(1)}, f32[1,1,1,8,1,8,1024]{6,5,3,2,1,4,0:T(8,128)S(1)}, u32[]{:S(2)}, u32[]{:S(2)}) collective-permute-start(f32[1,1,1,8,1,8,1024]{6,5,3,2,1,4,0:T(8,128)S(1)} %constant_dynamic-slice_fusion.10), channel_id=1, source_target_pairs={{0,16},{8,24},{16,0},{24,8},{1,17},{9,25},{17,1},{25,9},{2,18},{10... | collective-permute-start | bytes 786440 | tf_op jit(solution)/shard_map/ppermute | solution.py:57
  26.1 6.6 %collective-permute-start.8 = (bf16[1,1,1,32,1024]{4,3,2,1,0:T(8,128)(2,1)S(1)}, bf16[1,1,1,32,1024]{4,3,2,1,0:T(8,128)(2,1)S(1)}, u32[]{:S(2)}, u32[]{:S(2)}) collective-permute-start(bf16[1,1,1,32,1024]{4,3,2,1,0:T(8,128)(2,1)S(1)} %constant_dynamic-slice_fusion.8), channel_id=1, source_target_pairs={{0,4},{1,5},{2,6},{3,7},{4,0},{5,1},{6,2},{7,3},{8,12},{9,13},{10,... | collective-permute-start | bytes 196616 | tf_op jit(solution)/shard_map/ppermute | solution.py:57
  44.8 10.4 %collective-permute-start.11 = (bf16[1,1,1,8,32,1024]{5,4,3,2,1,0:T(8,128)(2,1)S(1)}, bf16[1,1,1,8,32,1024]{5,4,3,2,1,0:T(8,128)(2,1)S(1)}, u32[]{:S(2)}, u32[]{:S(2)}) collective-permute-start(bf16[1,1,1,8,32,1024]{5,4,3,2,1,0:T(8,128)(2,1)S(1)} %constant_dynamic-slice_fusion.5), channel_id=1, source_target_pairs={{0,16},{8,24},{16,0},{24,8},{1,17},{9,25},{17,1},{25,9},{2,18},{10... | collective-permute-start | bytes 1572872 | tf_op jit(solution)/shard_map/ppermute | solution.py:57
  56.4 65.8 %collective-permute-start.12 = (bf16[2,1,1,8,32,1024]{5,4,3,1,0,2:T(8,128)(2,1)}, bf16[2,1,1,8,32,1024]{5,4,3,1,0,2:T(8,128)(2,1)}, u32[]{:S(2)}, u32[]{:S(2)}) collective-permute-start(bf16[2,1,1,8,32,1024]{5,4,3,1,0,2:T(8,128)(2,1)} %constant_dynamic-slice_fusion.4), channel_id=1, source_target_pairs={{0,8},{8,0},{16,24},{24,16},{1,9},{9,1},{17,25},{25,17},{2,10},{10... | collective-permute-start | bytes 3145736 | tf_op jit(solution)/shard_map/ppermute | solution.py:57
  56.5 12.4 %collective-permute-start = (bf16[3,8,8192]{2,1,0:T(8,128)(2,1)S(1)}, bf16[3,8,8192]{2,1,0:T(8,128)(2,1)S(1)}, u32[]{:S(2)}, u32[]{:S(2)}) collective-permute-start(bf16[3,8,8192]{2,1,0:T(8,128)(2,1)S(1)} %pad_maximum_fusion.1), channel_id=1, source_target_pairs={{0,1},{1,2},{2,3},{3,4},{4,5},{5,6},{6,7},{8,9},{9,10},{10,11},{11... | collective-permute-start | bytes 1179656 | tf_op jit(solution)/shard_map/ppermute | solution.py:201
  76.5 40.6 %collective-permute-start.17 = (bf16[128,2048]{1,0:T(8,128)(2,1)}, bf16[128,2048]{1,0:T(8,128)(2,1)S(1)}, u32[]{:S(2)}, u32[]{:S(2)}) collective-permute-start(bf16[128,2048]{1,0:T(8,128)(2,1)} %get-tuple-element.52.refs_6_), channel_id=1, source_target_pairs={{0,1},{1,2},{2,3},{3,4},{4,5},{5,6},{6,7},{8,9},{9,10},{10,11},{11... | collective-permute-start | bytes 1572872 | tf_op jit(solution)/shard_map/ppermute | solution.py:232
  82.0 43.8 %collective-permute-start.18 = (bf16[128,2048]{1,0:T(8,128)(2,1)}, bf16[128,2048]{1,0:T(8,128)(2,1)}, u32[]{:S(2)}, u32[]{:S(2)}) collective-permute-start(bf16[128,2048]{1,0:T(8,128)(2,1)} %get-tuple-element.53.refs_8_), channel_id=1, source_target_pairs={{1,0},{2,1},{3,2},{4,3},{5,4},{6,5},{7,6},{9,8},{10,9},{11,10},{12... | collective-permute-start | bytes 1572872 | tf_op jit(solution)/shard_map/ppermute | solution.py:232
  90.2 57.9 %collective-permute-start.15 = (bf16[128,2048]{1,0:T(8,128)(2,1)}, bf16[128,2048]{1,0:T(8,128)(2,1)S(1)}, u32[]{:S(2)}, u32[]{:S(2)}) collective-permute-start(bf16[128,2048]{1,0:T(8,128)(2,1)} %get-tuple-element.50.refs_6_), channel_id=1, source_target_pairs={{0,1},{1,2},{2,3},{3,4},{4,5},{5,6},{6,7},{8,9},{9,10},{10,11},{11... | collective-permute-start | bytes 1572872 | tf_op jit(solution)/shard_map/ppermute | solution.py:232
  96.1 51.9 %collective-permute-start.16 = (bf16[128,2048]{1,0:T(8,128)(2,1)}, bf16[128,2048]{1,0:T(8,128)(2,1)}, u32[]{:S(2)}, u32[]{:S(2)}) collective-permute-start(bf16[128,2048]{1,0:T(8,128)(2,1)} %get-tuple-element.51.refs_8_), channel_id=1, source_target_pairs={{1,0},{2,1},{3,2},{4,3},{5,4},{6,5},{7,6},{9,8},{10,9},{11,10},{12... | collective-permute-start | bytes 1572872 | tf_op jit(solution)/shard_map/ppermute | solution.py:232
  117.9 49.3 %collective-permute-start.13 = (bf16[128,2048]{1,0:T(8,128)(2,1)}, bf16[128,2048]{1,0:T(8,128)(2,1)S(1)}, u32[]{:S(2)}, u32[]{:S(2)}) collective-permute-start(bf16[128,2048]{1,0:T(8,128)(2,1)} %get-tuple-element.48.refs_6_), channel_id=1, source_target_pairs={{0,1},{1,2},{2,3},{3,4},{4,5},{5,6},{6,7},{8,9},{9,10},{10,11},{11... | collective-permute-start | bytes 1572872 | tf_op jit(solution)/shard_map/ppermute | solution.py:232
  122.2 45.0 %collective-permute-start.14 = (bf16[128,2048]{1,0:T(8,128)(2,1)}, bf16[128,2048]{1,0:T(8,128)(2,1)}, u32[]{:S(2)}, u32[]{:S(2)}) collective-permute-start(bf16[128,2048]{1,0:T(8,128)(2,1)} %get-tuple-element.49.refs_8_), channel_id=1, source_target_pairs={{1,0},{2,1},{3,2},{4,3},{5,4},{6,5},{7,6},{9,8},{10,9},{11,10},{12... | collective-permute-start | bytes 1572872 | tf_op jit(solution)/shard_map/ppermute | solution.py:232
  189.7 71.4 %collective-permute-start.21 = (f32[2,8,40,768]{3,2,1,0:T(8,128)}, f32[2,8,40,768]{3,2,1,0:T(8,128)}, u32[]{:S(2)}, u32[]{:S(2)}) collective-permute-start(f32[2,8,40,768]{3,2,1,0:T(8,128)} %dynamic-slice_bitcast_fusion), channel_id=1, source_target_pairs={{0,8},{8,0},{16,24},{24,16},{1,9},{9,1},{17,25},{25,17},{2,10},{10... | collective-permute-start | bytes 5898248 | tf_op jit(solution)/shard_map/ppermute | solution.py:57
  196.7 34.1 %collective-permute-start.6 = (bf16[128,2048]{1,0:T(8,128)(2,1)}, bf16[128,2048]{1,0:T(8,128)(2,1)S(1)}, u32[]{:S(2)}, u32[]{:S(2)}) collective-permute-start(bf16[128,2048]{1,0:T(8,128)(2,1)} %get-tuple-element.45.refs_6_), channel_id=1, source_target_pairs={{0,1},{1,2},{2,3},{3,4},{4,5},{5,6},{6,7},{8,9},{9,10},{10,11},{11... | collective-permute-start | bytes 1572872 | tf_op jit(solution)/shard_map/ppermute | solution.py:232
  201.5 29.4 %collective-permute-start.7 = (bf16[128,2048]{1,0:T(8,128)(2,1)}, bf16[128,2048]{1,0:T(8,128)(2,1)S(1)}, u32[]{:S(2)}, u32[]{:S(2)}) collective-permute-start(bf16[128,2048]{1,0:T(8,128)(2,1)} %get-tuple-element.46.refs_8_), channel_id=1, source_target_pairs={{1,0},{2,1},{3,2},{4,3},{5,4},{6,5},{7,6},{9,8},{10,9},{11,10},{12... | collective-permute-start | bytes 1572872 | tf_op jit(solution)/shard_map/ppermute | solution.py:232
  204.5 48.3 %collective-permute-start.19 = (bf16[9,8,2048]{2,1,0:T(8,128)(2,1)}, bf16[9,8,2048]{2,1,0:T(8,128)(2,1)}, u32[]{:S(2)}, u32[]{:S(2)}) collective-permute-start(bf16[9,8,2048]{2,1,0:T(8,128)(2,1)} %pad_maximum_fusion.2), channel_id=1, source_target_pairs={{1,0},{2,1},{3,2},{4,3},{5,4},{6,5},{7,6},{9,8},{10,9},{11,10},{12... | collective-permute-start | bytes 884744 | tf_op jit(solution)/shard_map/ppermute | solution.py:282
  251.4 8.0 %collective-permute-start.26 = (f32[2,8,40,256]{3,2,1,0:T(8,128)S(1)}, f32[2,8,40,256]{3,2,1,0:T(8,128)S(1)}, u32[]{:S(2)}, u32[]{:S(2)}) collective-permute-start(f32[2,8,40,256]{3,2,1,0:T(8,128)S(1)} %dynamic-slice_bitcast_fusion.1), channel_id=1, source_target_pairs={{0,8},{8,0},{16,24},{24,16},{1,9},{9,1},{17,25},{25,17},{2,10},{10... | collective-permute-start | bytes 1966088 | tf_op jit(solution)/shard_map/ppermute | solution.py:57
  251.5 7.7 %collective-permute-start.20 = (bf16[3,8,2048]{2,1,0:T(8,128)(2,1)S(1)}, bf16[3,8,2048]{2,1,0:T(8,128)(2,1)S(1)}, u32[]{:S(2)}, u32[]{:S(2)}) collective-permute-start(bf16[3,8,2048]{2,1,0:T(8,128)(2,1)S(1)} %get-tuple-element.75), channel_id=1, source_target_pairs={{1,0},{2,1},{3,2},{4,3},{5,4},{6,5},{7,6},{9,8},{10,9},{11,10},{12... | collective-permute-start | bytes 294920 | tf_op jit(solution)/shard_map/ppermute | solution.py:282
  263.2 13.1 %collective-permute-start.22 = (bf16[1,8,40,768]{3,2,1,0:T(8,128)(2,1)S(1)}, bf16[1,8,40,768]{3,2,1,0:T(8,128)(2,1)S(1)}, u32[]{:S(2)}, u32[]{:S(2)}) collective-permute-start(bf16[1,8,40,768]{3,2,1,0:T(8,128)(2,1)S(1)} %dynamic-slice_convert_fusion), channel_id=1, source_target_pairs={{0,16},{8,24},{16,0},{24,8},{1,17},{9,25},{17,1},{25,9},{2,18},{10... | collective-permute-start | bytes 1474568 | tf_op jit(solution)/shard_map/ppermute | solution.py:57
  265.7 13.3 %collective-permute-start.28 = (bf16[4,40,256]{2,1,0:T(8,128)(2,1)S(1)}, bf16[4,40,256]{2,1,0:T(8,128)(2,1)S(1)}, u32[]{:S(2)}, u32[]{:S(2)}) collective-permute-start(bf16[4,40,256]{2,1,0:T(8,128)(2,1)S(1)} %fusion.4), channel_id=1, source_target_pairs={{0,1},{1,0},{2,3},{3,2},{4,5},{5,4},{6,7},{7,6},{8,9},{9,8},{10,11... | collective-permute-start | bytes 245768 | tf_op jit(solution)/shard_map/ppermute | solution.py:57
  276.4 7.4 %collective-permute-start.23 = (bf16[4,40,768]{2,1,0:T(8,128)(2,1)S(1)}, bf16[4,40,768]{2,1,0:T(8,128)(2,1)S(1)}, u32[]{:S(2)}, u32[]{:S(2)}) collective-permute-start(bf16[4,40,768]{2,1,0:T(8,128)(2,1)S(1)} %fusion.1), channel_id=1, source_target_pairs={{0,1},{1,0},{2,3},{3,2},{4,5},{5,4},{6,7},{7,6},{8,9},{9,8},{10,11... | collective-permute-start | bytes 737288 | tf_op jit(solution)/shard_map/ppermute | solution.py:57
  279.0 7.8 %collective-permute-start.29 = (f32[2,40,256]{2,1,0:T(8,128)S(1)}, f32[2,40,256]{2,1,0:T(8,128)S(1)}, u32[]{:S(2)}, u32[]{:S(2)}) collective-permute-start(f32[2,40,256]{2,1,0:T(8,128)S(1)} %dynamic-slice_bitcast_fusion.3), channel_id=1, source_target_pairs={{0,2},{1,3},{2,0},{3,1},{4,6},{5,7},{6,4},{7,5},{8,10},{9,11},{10,... | collective-permute-start | bytes 245768 | tf_op jit(solution)/shard_map/ppermute | solution.py:57
  283.9 7.9 %collective-permute-start.24 = (f32[2,40,768]{2,1,0:T(8,128)S(1)}, f32[2,40,768]{2,1,0:T(8,128)S(1)}, u32[]{:S(2)}, u32[]{:S(2)}) collective-permute-start(f32[2,40,768]{2,1,0:T(8,128)S(1)} %dynamic-slice_bitcast_fusion.2), channel_id=1, source_target_pairs={{0,2},{1,3},{2,0},{3,1},{4,6},{5,7},{6,4},{7,5},{8,10},{9,11},{10,... | collective-permute-start | bytes 737288 | tf_op jit(solution)/shard_map/ppermute | solution.py:57
  286.9 9.7 %collective-permute-start.30 = (f32[1,40,256]{2,1,0:T(8,128)S(1)}, f32[1,40,256]{2,1,0:T(8,128)S(1)}, u32[]{:S(2)}, u32[]{:S(2)}) collective-permute-start(f32[1,40,256]{2,1,0:T(8,128)S(1)} %constant_dynamic-slice_fusion.2), channel_id=1, source_target_pairs={{0,4},{1,5},{2,6},{3,7},{4,0},{5,1},{6,2},{7,3},{8,12},{9,13},{10,... | collective-permute-start | bytes 122888 | tf_op jit(solution)/shard_map/ppermute | solution.py:57
  291.9 8.0 %collective-permute-start.25 = (f32[1,40,768]{2,1,0:T(8,128)S(1)}, f32[1,40,768]{2,1,0:T(8,128)S(1)}, u32[]{:S(2)}, u32[]{:S(2)}) collective-permute-start(f32[1,40,768]{2,1,0:T(8,128)S(1)} %constant_dynamic-slice_fusion.3), channel_id=1, source_target_pairs={{0,4},{1,5},{2,6},{3,7},{4,0},{5,1},{6,2},{7,3},{8,12},{9,13},{10,... | collective-permute-start | bytes 368648 | tf_op jit(solution)/shard_map/ppermute | solution.py:57
  (38 other events, 382.8 us)

commit v3 on v2

--- a/solution.py
+++ b/solution.py
@@ -57,7 +57,8 @@
     return lax.ppermute(x, axis, [(i, i ^ (1 << bit)) for i in range(count)])
 
 
-def gather(block, axis, count):
+def gather(block, axis, count, after=()):
+    after = list(after)
     me = lax.axis_index(axis)
     rest = block.shape
     zeros = (0,) * len(rest)
@@ -67,6 +68,8 @@
         view = held.reshape((count // (2 * low), 2, low) + rest)
         mine = (me // low) % 2
         own = lax.dynamic_slice(view, (0, mine, me % low) + zeros, (count // (2 * low), 1, 1) + rest)
+        if after:
+            own, _ = lax.optimization_barrier((own, after.pop(0)))
         other = swap(own, axis, count, bit)
         view = lax.dynamic_update_slice(view, other, (0, 1 - mine, me % low) + zeros)
         held = view.reshape((count,) + rest)
@@ -180,9 +183,9 @@
     width = short_filter.shape[2]
     chans = full // n_ctx
     share = med_filter.shape[1]
-    pieces = max(1, min(4, chans // 128))
+    pieces = max(1, min(2, chans // 128))
     part = chans // pieces
-    cb = 256 if part % 256 == 0 else 128
+    cb = 512 if part % 512 == 0 else 128
     inner = part // cb
     per = -(-3 // n_dp)
     slot = HALO * per
@@ -193,8 +196,6 @@
     shorts = jnp.pad(short_filter.transpose(0, 2, 1), ((0, n_dp * per - 3), (0, HALO - width), (0, 0)))
     shorts = lax.dynamic_slice_in_dim(shorts, lax.axis_index("dp") * per, per, 0)
     shorts = gather(gather(shorts, "context", n_ctx), "dp", n_dp)
-    taps, shorts = lax.optimization_barrier((med_filter.astype(BF).T, shorts))
-    taps = gather(gather(taps, "context", n_ctx), "dp", n_dp)
     table = jnp.asarray(tables(length))
 
     rim = jnp.stack([a[length - HALO :] for a in (q, k, v)])
@@ -228,6 +229,9 @@
                 name="featurize",
             )(q, k, v, g, rims, shorts)
         )
+    done = [u for u, _ in sent]
+    taps = gather(med_filter.astype(BF).T, "context", n_ctx)
+    taps = gather(taps, "dp", n_dp, done[:1])
     arrived = [
         (lax.ppermute(u, "context", right), lax.ppermute(d, "context", left)) for u, d in sent
     ]
@@ -242,6 +246,9 @@
         args = [q, k, v, g, rims, shorts, sent[c][0], arrived[c][0], sent[c][1], arrived[c][1], taps, table]
         specs = [whole(c)] * 4 + [edge(c), short_spec(c)] + [piece] * 4 + [tap_spec, table_spec]
         alias = {}
+        if c == 0:
+            args.append(done[-1])
+            specs.append(pl.BlockSpec(memory_space=pl.ANY))
         if grown is not None:
             alias = {len(args) + i: i for i in range(4)}
             args += grown
@@ -274,9 +281,10 @@
     def reduce(items):
         x = jnp.concatenate(items, axis=3) if len(items) > 1 else items[0]
         x = scatter_sum(x, "dp", n_dp, (1,))
-        return scatter_sum(x, "context", n_ctx, (0,))
-
-    groups = [(0, pieces - 1), (pieces - 1, pieces)] if pieces > 1 else [(0, 1)]
+        return scatter_sum(x, "context", n_ctx, bits_of(n_ctx))
+
+    half = pieces // 2
+    groups = [(0, half), (half, pieces)] if pieces > 1 else [(0, 1)]
     sums = [reduce(sums[a:b]) for a, b in groups]
     heads = [
         h for a, b in groups for h in jnp.split(lax.ppermute(jnp.concatenate(heads[a:b], axis=0), "context", left), b - a)

time: 308 us -> 259 us (0.84)
  starting transfers between devices: 69.8 us -> 55.7 us
  Pallas kernels: 101 us -> 87.1 us
  waiting for transfers between devices: 108 us -> 95.9 us
  local copies, waits for them, and re-layouts: 20.6 us -> 14 us
    ppermute x22, waiting for transfers between devices: 55.7 us -> 36.3 us  [swap(): return lax.ppermute(x, axis, [(i, i ^ 1 << bit) for i in range(count)])]
    ppermute x4 -> x2, starting transfers between devices: 20.5 us -> 11 us  [per_device(): lax.ppermute(u, 'context', right)]
    unnamed x52 -> x26, local copies, waits for them, and re-layouts: 10.5 us -> 2.36 us
    ppermute x4 -> x2, waiting for transfers between devices: 37.7 us -> 45.9 us  [per_device(): lax.ppermute(u, 'context', right)]
    pallas_call x4 -> x2, Pallas kernels: 73.7 us -> 65.8 us  [per_device(): pl.pallas_call(functools.partial(second_kernel, width), grid=(n_ctx, inne...]
    pallas_call x4 -> x2, Pallas kernels: 27.6 us -> 21.3 us  [per_device(): pl.pallas_call(functools.partial(first_kernel, width), grid=(n_ctx, inner...]
    ppermute x1, waiting for transfers between devices: 8.99 us -> 5.42 us  [per_device(): rims = lax.ppermute(rim, 'context', right)]
  transfers between devices with their start and end apart: 33 -> 29, of which waited for: 20 -> 17; matrix products, arithmetic and copies ran while one was open for 3% -> 5% of each run, Pallas kernels for 27% -> 17%
where the time goes in v3:
time: 259 us; the launch traced here: 258 us
  waiting for transfers between devices  95.9 us (37%)
  Pallas kernels  87.1 us (34%)
  starting transfers between devices  55.7 us (22%)
  local copies, waits for them, and re-layouts  14 us (5%)
  other arithmetic  3.37 us (1%)
    pallas_call x2, Pallas kernels, per_device(): pl.pallas_call(functools.partial(second_kernel, width), grid=(n_ctx, inne...  65.8 us
    ppermute x2, waiting for transfers between devices, per_device(): lax.ppermute(u, 'context', right)  45.9 us
    ppermute x22, waiting for transfers between devices, swap(): return lax.ppermute(x, axis, [(i, i ^ 1 << bit) for i in range(count)])  36.3 us
    ppermute x22, starting transfers between devices, swap(): return lax.ppermute(x, axis, [(i, i ^ 1 << bit) for i in range(count)])  35.7 us
    pallas_call x2, Pallas kernels, per_device(): pl.pallas_call(functools.partial(first_kernel, width), grid=(n_ctx, inner...  21.3 us
    ppermute x2, starting transfers between devices, per_device(): lax.ppermute(u, 'context', right)  11 us
    ppermute x2, waiting for transfers between devices, per_device(): lax.ppermute(jnp.concatenate(heads[a:b], axis=0), 'context', left)  8.3 us
    ppermute x1, waiting for transfers between devices, per_device(): rims = lax.ppermute(rim, 'context', right)  5.42 us
  transfers between devices with their start and end apart: 29, of which 17 were waited for; matrix products, arithmetic and copies ran while one was open for 5% of the time, Pallas kernels for 17%

profile of v3, /device:TPU:0, one launch (start us, length us, event | category | flops | bytes accessed | tf_op | source)
XLA Modules:
  0.0 257.6 jit_solution(6543912567172874228)
XLA Ops:
  1.5 4.1 %collective-permute-start.1 = (f32[1,1,1,1,8,1024]{5,4,2,1,3,0:T(8,128)S(1)}, f32[1,1,1,1,8,1024]{5,4,2,1,3,0:T(8,128)S(1)}, u32[]{:S(2)}, u32[]{:S(2)}) collective-permute-start(f32[1,1,1,1,8,1024]{5,4,2,1,3,0:T(8,128)S(1)} %constant_dynamic-slice_fusion.11), channel_id=1, source_target_pairs={{0,4},{1,5},{2,6},{3,7},{4,0},{5,1},{6,2},{7,3},{8,12},{9,13},{10,... | collective-permute-start | bytes 98312 | tf_op jit(solution)/shard_map/ppermute | solution.py:57
  9.5 2.8 %collective-permute-start.8 = (bf16[1,1,1,32,1024]{4,3,2,1,0:T(8,128)(2,1)S(1)}, bf16[1,1,1,32,1024]{4,3,2,1,0:T(8,128)(2,1)S(1)}, u32[]{:S(2)}, u32[]{:S(2)}) collective-permute-start(bf16[1,1,1,32,1024]{4,3,2,1,0:T(8,128)(2,1)S(1)} %constant_dynamic-slice_fusion.6), channel_id=1, source_target_pairs={{0,4},{1,5},{2,6},{3,7},{4,0},{5,1},{6,2},{7,3},{8,12},{9,13},{10,... | collective-permute-start | bytes 196616 | tf_op jit(solution)/shard_map/ppermute | solution.py:57
  22.0 2.4 collective-permute-done.4
  26.1 3.5 %collective-permute-start = (bf16[3,8,8192]{2,1,0:T(8,128)(2,1)}, bf16[3,8,8192]{2,1,0:T(8,128)(2,1)S(1)}, u32[]{:S(2)}, u32[]{:S(2)}) collective-permute-start(bf16[3,8,8192]{2,1,0:T(8,128)(2,1)} %pad_maximum_fusion), channel_id=1, source_target_pairs={{0,1},{1,2},{2,3},{3,4},{4,5},{5,6},{6,7},{8,9},{9,10},{10,11},{11... | collective-permute-start | bytes 1179656 | tf_op jit(solution)/shard_map/ppermute | solution.py:202
  33.5 5.4 %collective-permute-done.halo_ref.refs_4_ = bf16[3,8,8192]{2,1,0:T(8,128)(2,1)S(1)} collective-permute-done((bf16[3,8,8192]{2,1,0:T(8,128)(2,1)}, bf16[3,8,8192]{2,1,0:T(8,128)(2,1)S(1)}, u32[]{:S(2)}, u32[]{:S(2)}) %collective-permute-start) | collective-permute-done | bytes 393248 | tf_op jit(solution)/shard_map/ppermute | solution.py:202
  39.7 10.7 %featurize.3 = (bf16[128,4096]{1,0:T(8,128)(2,1)}, bf16[128,4096]{1,0:T(8,128)(2,1)}) custom-call(bf16[128,8192]{1,0:T(8,128)(2,1)} %bitcast.103, bf16[128,8192]{1,0:T(8,128)(2,1)} %bitcast.107, bf16[128,8192]{1,0:T(8,128)(2,1)} %bitcast.111, bf16[128,8192]{1,0:T(8,128)(2,1)} %bitcast.115, bf16[3,8,8192]{2,1,0:T(8,128)(2,1)} %copy-done.2, ...), custom_call_target="tpu_custom_call" | custom-call | flops 26214400 | bytes 12582912 | tf_op jit(solution)/shard_map/featurize/pallas_call | solution.py:219
  51.5 12.7 %collective-permute-done.11 = bf16[1,1,1,8,32,1024]{5,4,3,2,1,0:T(8,128)(2,1)S(1)} collective-permute-done((bf16[1,1,1,8,32,1024]{5,4,3,2,1,0:T(8,128)(2,1)}, bf16[1,1,1,8,32,1024]{5,4,3,2,1,0:T(8,128)(2,1)S(1)}, u32[]{:S(2)}, u32[]{:S(2)}) %collective-permute-start.11) | collective-permute-done | bytes 524320 | tf_op jit(solution)/shard_map/ppermute | solution.py:57
  65.4 5.3 %collective-permute-start.13 = (bf16[128,4096]{1,0:T(8,128)(2,1)S(1)}, bf16[128,4096]{1,0:T(8,128)(2,1)}, u32[]{:S(2)}, u32[]{:S(2)}) collective-permute-start(bf16[128,4096]{1,0:T(8,128)(2,1)S(1)} %copy-done.6), channel_id=1, source_target_pairs={{0,1},{1,2},{2,3},{3,4},{4,5},{5,6},{6,7},{8,9},{9,10},{10,11},{11... | collective-permute-start | bytes 3145736 | tf_op jit(solution)/shard_map/ppermute | solution.py:236
  72.0 10.7 %featurize.2 = (bf16[128,4096]{1,0:T(8,128)(2,1)}, bf16[128,4096]{1,0:T(8,128)(2,1)}) custom-call(bf16[128,8192]{1,0:T(8,128)(2,1)} %bitcast.104, bf16[128,8192]{1,0:T(8,128)(2,1)} %bitcast.108, bf16[128,8192]{1,0:T(8,128)(2,1)} %bitcast.112, bf16[128,8192]{1,0:T(8,128)(2,1)} %bitcast.116, bf16[3,8,8192]{2,1,0:T(8,128)(2,1)} %copy-done.2, ...), custom_call_target="tpu_custom_call" | custom-call | flops 26214400 | bytes 12582912 | tf_op jit(solution)/shard_map/featurize/pallas_call | solution.py:219
  82.7 5.7 %collective-permute-start.6 = (bf16[128,4096]{1,0:T(8,128)(2,1)}, bf16[128,4096]{1,0:T(8,128)(2,1)}, u32[]{:S(2)}, u32[]{:S(2)}) collective-permute-start(bf16[128,4096]{1,0:T(8,128)(2,1)} %get-tuple-element.25.refs_12_.refs_6_), channel_id=1, source_target_pairs={{0,1},{1,2},{2,3},{3,4},{4,5},{5,6},{6,7},{8,9},{9,10},{10,11},{11... | collective-permute-start | bytes 3145736 | tf_op jit(solution)/shard_map/ppermute | solution.py:236
  89.9 2.3 constant_dynamic-update-slice_fusion.4
  92.2 45.9 %collective-permute-done.13.refs_7_ = bf16[128,4096]{1,0:T(8,128)(2,1)} collective-permute-done((bf16[128,4096]{1,0:T(8,128)(2,1)S(1)}, bf16[128,4096]{1,0:T(8,128)(2,1)}, u32[]{:S(2)}, u32[]{:S(2)}) %collective-permute-start.13) | collective-permute-done | bytes 1048608 | tf_op jit(solution)/shard_map/ppermute | solution.py:236
  138.1 32.9 %mixer.2 = (bf16[128,8192]{1,0:T(8,128)(2,1)}, bf16[128,8192]{1,0:T(8,128)(2,1)}, bf16[128,8192]{1,0:T(8,128)(2,1)}, bf16[128,8192]{1,0:T(8,128)(2,1)}, f32[4,8,...) custom-call(bf16[128,8192]{1,0:T(8,128)(2,1)} %bitcast.105, ...), custom_call_target="tpu_custom_call" | custom-call | flops 2097152000 | bytes 41943040 | tf_op jit(solution)/shard_map/mixer/pallas_call | solution.py:256
  171.1 32.9 %mixer.3 = (bf16[128,8192]{1,0:T(8,128)(2,1)}, bf16[128,8192]{1,0:T(8,128)(2,1)}, bf16[128,8192]{1,0:T(8,128)(2,1)}, bf16[128,8192]{1,0:T(8,128)(2,1)}, f32[4,8,...) custom-call(bf16[128,8192]{1,0:T(8,128)(2,1)} %bitcast.106, ...), custom_call_target="tpu_custom_call", output_to_operand_aliasing={{0}: (12, {}), {1}: (13, {}), {2}: (14, {}), {3}: (15, {})} | custom-call | flops 2097152000 | bytes 41943040 | tf_op jit(solution)/shard_map/mixer/pallas_call | solution.py:256
  209.0 5.5 %collective-permute-done.16 = bf16[3,8,4096]{2,1,0:T(8,128)(2,1)S(1)} collective-permute-done((bf16[3,8,4096]{2,1,0:T(8,128)(2,1)S(1)}, bf16[3,8,4096]{2,1,0:T(8,128)(2,1)S(1)}, u32[]{:S(2)}, u32[]{:S(2)}) %collective-permute-start.16) | collective-permute-done | bytes 196640 | tf_op jit(solution)/shard_map/ppermute | solution.py:290
  214.5 2.8 %collective-permute-done.15 = bf16[3,8,4096]{2,1,0:T(8,128)(2,1)S(1)} collective-permute-done((bf16[3,8,4096]{2,1,0:T(8,128)(2,1)S(1)}, bf16[3,8,4096]{2,1,0:T(8,128)(2,1)S(1)}, u32[]{:S(2)}, u32[]{:S(2)}) %collective-permute-start.15) | collective-permute-done | bytes 196640 | tf_op jit(solution)/shard_map/ppermute | solution.py:290
  221.1 8.2 %collective-permute-done.23 = bf16[1,8,40,512]{3,2,1,0:T(8,128)(2,1)S(1)} collective-permute-done((bf16[1,8,40,512]{3,2,1,0:T(8,128)(2,1)S(1)}, bf16[1,8,40,512]{3,2,1,0:T(8,128)(2,1)S(1)}, u32[]{:S(2)}, u32[]{:S(2)}) %collective-permute-start.23) | collective-permute-done | bytes 327712 | tf_op jit(solution)/shard_map/ppermute | solution.py:57
  229.5 3.6 %collective-permute-start.24 = (bf16[4,40,512]{2,1,0:T(8,128)(2,1)S(1)}, bf16[4,40,512]{2,1,0:T(8,128)(2,1)S(1)}, u32[]{:S(2)}, u32[]{:S(2)}) collective-permute-start(bf16[4,40,512]{2,1,0:T(8,128)(2,1)S(1)} %fusion.2), channel_id=1, source_target_pairs={{0,1},{1,0},{2,3},{3,2},{4,5},{5,4},{6,7},{7,6},{8,9},{9,8},{10,11... | collective-permute-start | bytes 491528 | tf_op jit(solution)/shard_map/ppermute | solution.py:57
  234.2 4.2 %collective-permute-start.19 = (bf16[4,40,512]{2,1,0:T(8,128)(2,1)S(1)}, bf16[4,40,512]{2,1,0:T(8,128)(2,1)S(1)}, u32[]{:S(2)}, u32[]{:S(2)}) collective-permute-start(bf16[4,40,512]{2,1,0:T(8,128)(2,1)S(1)} %fusion.1), channel_id=1, source_target_pairs={{0,1},{1,0},{2,3},{3,2},{4,5},{5,4},{6,7},{7,6},{8,9},{9,8},{10,11... | collective-permute-start | bytes 491528 | tf_op jit(solution)/shard_map/ppermute | solution.py:57
  239.7 2.0 collective-permute-done.19
  241.8 2.2 collective-permute-start.20
  244.0 2.4 collective-permute-start.26
  246.4 3.1 %collective-permute-start.21 = (bf16[1,40,512]{2,1,0:T(8,128)(2,1)S(1)}, bf16[1,40,512]{2,1,0:T(8,128)(2,1)S(1)}, u32[]{:S(2)}, u32[]{:S(2)}) collective-permute-start(bf16[1,40,512]{2,1,0:T(8,128)(2,1)S(1)} %dynamic-slice_convert_fusion.6), channel_id=1, source_target_pairs={{0,4},{1,5},{2,6},{3,7},{4,0},{5,1},{6,2},{7,3},{8,12},{9,13},{10,... | collective-permute-start | bytes 122888 | tf_op jit(solution)/shard_map/ppermute | solution.py:57
  249.5 2.0 collective-permute-done.21
  (135 shorter events, 43.2 us)
Async XLA Ops:
  1.5 6.3 %collective-permute-start.1 = (f32[1,1,1,1,8,1024]{5,4,2,1,3,0:T(8,128)S(1)}, f32[1,1,1,1,8,1024]{5,4,2,1,3,0:T(8,128)S(1)}, u32[]{:S(2)}, u32[]{:S(2)}) collective-permute-start(f32[1,1,1,1,8,1024]{5,4,2,1,3,0:T(8,128)S(1)} %constant_dynamic-slice_fusion.11), channel_id=1, source_target_pairs={{0,4},{1,5},{2,6},{3,7},{4,0},{5,1},{6,2},{7,3},{8,12},{9,13},{10,... | collective-permute-start | bytes 98312 | tf_op jit(solution)/shard_map/ppermute | solution.py:57
  9.5 5.9 %collective-permute-start.8 = (bf16[1,1,1,32,1024]{4,3,2,1,0:T(8,128)(2,1)S(1)}, bf16[1,1,1,32,1024]{4,3,2,1,0:T(8,128)(2,1)S(1)}, u32[]{:S(2)}, u32[]{:S(2)}) collective-permute-start(bf16[1,1,1,32,1024]{4,3,2,1,0:T(8,128)(2,1)S(1)} %constant_dynamic-slice_fusion.6), channel_id=1, source_target_pairs={{0,4},{1,5},{2,6},{3,7},{4,0},{5,1},{6,2},{7,3},{8,12},{9,13},{10,... | collective-permute-start | bytes 196616 | tf_op jit(solution)/shard_map/ppermute | solution.py:57
  12.7 5.0 %collective-permute-start.3 = (f32[4,1,1,1,8,1024]{5,4,1,0,3,2:T(8,128)S(1)}, f32[4,1,1,1,8,1024]{5,4,1,0,3,2:T(8,128)S(1)}, u32[]{:S(2)}, u32[]{:S(2)}) collective-permute-start(f32[4,1,1,1,8,1024]{5,4,1,0,3,2:T(8,128)S(1)} %constant_dynamic-slice_fusion.9), channel_id=1, source_target_pairs={{0,1},{1,0},{2,3},{3,2},{4,5},{5,4},{6,7},{7,6},{8,9},{9,8},{10,11... | collective-permute-start | bytes 393224 | tf_op jit(solution)/shard_map/ppermute | solution.py:57
  18.0 6.4 %collective-permute-start.4 = (f32[1,1,1,8,1,8,1024]{6,5,3,2,1,4,0:T(8,128)S(1)}, f32[1,1,1,8,1,8,1024]{6,5,3,2,1,4,0:T(8,128)S(1)}, u32[]{:S(2)}, u32[]{:S(2)}) collective-permute-start(f32[1,1,1,8,1,8,1024]{6,5,3,2,1,4,0:T(8,128)S(1)} %constant_dynamic-slice_fusion.8), channel_id=1, source_target_pairs={{0,16},{8,24},{16,0},{24,8},{1,17},{9,25},{17,1},{25,9},{2,18},{10... | collective-permute-start | bytes 786440 | tf_op jit(solution)/shard_map/ppermute | solution.py:57
  20.5 9.2 %collective-permute-start.10 = (bf16[4,1,1,32,1024]{4,3,1,0,2:T(8,128)(2,1)S(1)}, bf16[4,1,1,32,1024]{4,3,1,0,2:T(8,128)(2,1)S(1)}, u32[]{:S(2)}, u32[]{:S(2)}) collective-permute-start(bf16[4,1,1,32,1024]{4,3,1,0,2:T(8,128)(2,1)S(1)} %constant_dynamic-slice_fusion.4), channel_id=1, source_target_pairs={{0,1},{1,0},{2,3},{3,2},{4,5},{5,4},{6,7},{7,6},{8,9},{9,8},{10,11... | collective-permute-start | bytes 786440 | tf_op jit(solution)/shard_map/ppermute | solution.py:57
  25.3 7.1 %collective-permute-start.5 = (f32[2,1,1,8,1,8,1024]{6,5,3,1,0,4,2:T(8,128)}, f32[2,1,1,8,1,8,1024]{6,5,3,1,0,4,2:T(8,128)}, u32[]{:S(2)}, u32[]{:S(2)}) collective-permute-start(f32[2,1,1,8,1,8,1024]{6,5,3,1,0,4,2:T(8,128)} %constant_dynamic-slice_fusion.7), channel_id=1, source_target_pairs={{0,8},{8,0},{16,24},{24,16},{1,9},{9,1},{17,25},{25,17},{2,10},{10... | collective-permute-start | bytes 1572872 | tf_op jit(solution)/shard_map/ppermute | solution.py:57
  26.1 12.8 %collective-permute-start = (bf16[3,8,8192]{2,1,0:T(8,128)(2,1)}, bf16[3,8,8192]{2,1,0:T(8,128)(2,1)S(1)}, u32[]{:S(2)}, u32[]{:S(2)}) collective-permute-start(bf16[3,8,8192]{2,1,0:T(8,128)(2,1)} %pad_maximum_fusion), channel_id=1, source_target_pairs={{0,1},{1,2},{2,3},{3,4},{4,5},{5,6},{6,7},{8,9},{9,10},{10,11},{11... | collective-permute-start | bytes 1179656 | tf_op jit(solution)/shard_map/ppermute | solution.py:202
  50.3 13.8 %collective-permute-start.11 = (bf16[1,1,1,8,32,1024]{5,4,3,2,1,0:T(8,128)(2,1)}, bf16[1,1,1,8,32,1024]{5,4,3,2,1,0:T(8,128)(2,1)S(1)}, u32[]{:S(2)}, u32[]{:S(2)}) collective-permute-start(bf16[1,1,1,8,32,1024]{5,4,3,2,1,0:T(8,128)(2,1)} %constant_dynamic-slice_fusion.3), channel_id=1, source_target_pairs={{0,16},{8,24},{16,0},{24,8},{1,17},{9,25},{17,1},{25,9},{2,18},{10... | collective-permute-start | bytes 1572872 | tf_op jit(solution)/shard_map/ppermute | solution.py:57
  65.4 24.5 %collective-permute-start.12 = (bf16[2,1,1,8,32,1024]{5,4,3,1,0,2:T(8,128)(2,1)}, bf16[2,1,1,8,32,1024]{5,4,3,1,0,2:T(8,128)(2,1)}, u32[]{:S(2)}, u32[]{:S(2)}) collective-permute-start(bf16[2,1,1,8,32,1024]{5,4,3,1,0,2:T(8,128)(2,1)} %constant_dynamic-slice_fusion.2), channel_id=1, source_target_pairs={{0,8},{8,0},{16,24},{24,16},{1,9},{9,1},{17,25},{25,17},{2,10},{10... | collective-permute-start | bytes 3145736 | tf_op jit(solution)/shard_map/ppermute | solution.py:57
  65.4 72.7 %collective-permute-start.13 = (bf16[128,4096]{1,0:T(8,128)(2,1)S(1)}, bf16[128,4096]{1,0:T(8,128)(2,1)}, u32[]{:S(2)}, u32[]{:S(2)}) collective-permute-start(bf16[128,4096]{1,0:T(8,128)(2,1)S(1)} %copy-done.6), channel_id=1, source_target_pairs={{0,1},{1,2},{2,3},{3,4},{4,5},{5,6},{6,7},{8,9},{9,10},{10,11},{11... | collective-permute-start | bytes 3145736 | tf_op jit(solution)/shard_map/ppermute | solution.py:236
  70.7 67.4 %collective-permute-start.14 = (bf16[128,4096]{1,0:T(8,128)(2,1)}, bf16[128,4096]{1,0:T(8,128)(2,1)}, u32[]{:S(2)}, u32[]{:S(2)}) collective-permute-start(bf16[128,4096]{1,0:T(8,128)(2,1)} %get-tuple-element.29.refs_8_), channel_id=1, source_target_pairs={{1,0},{2,1},{3,2},{4,3},{5,4},{6,5},{7,6},{9,8},{10,9},{11,10},{12... | collective-permute-start | bytes 3145736 | tf_op jit(solution)/shard_map/ppermute | solution.py:236
  82.7 88.4 %collective-permute-start.6 = (bf16[128,4096]{1,0:T(8,128)(2,1)}, bf16[128,4096]{1,0:T(8,128)(2,1)}, u32[]{:S(2)}, u32[]{:S(2)}) collective-permute-start(bf16[128,4096]{1,0:T(8,128)(2,1)} %get-tuple-element.25.refs_12_.refs_6_), channel_id=1, source_target_pairs={{0,1},{1,2},{2,3},{3,4},{4,5},{5,6},{6,7},{8,9},{9,10},{10,11},{11... | collective-permute-start | bytes 3145736 | tf_op jit(solution)/shard_map/ppermute | solution.py:236
  88.4 82.7 %collective-permute-start.7 = (bf16[128,4096]{1,0:T(8,128)(2,1)}, bf16[128,4096]{1,0:T(8,128)(2,1)}, u32[]{:S(2)}, u32[]{:S(2)}) collective-permute-start(bf16[128,4096]{1,0:T(8,128)(2,1)} %get-tuple-element.26.refs_8_), channel_id=1, source_target_pairs={{1,0},{2,1},{3,2},{4,3},{5,4},{6,5},{7,6},{9,8},{10,9},{11,10},{12... | collective-permute-start | bytes 3145736 | tf_op jit(solution)/shard_map/ppermute | solution.py:236
  203.9 10.6 %collective-permute-start.16 = (bf16[3,8,4096]{2,1,0:T(8,128)(2,1)S(1)}, bf16[3,8,4096]{2,1,0:T(8,128)(2,1)S(1)}, u32[]{:S(2)}, u32[]{:S(2)}) collective-permute-start(bf16[3,8,4096]{2,1,0:T(8,128)(2,1)S(1)} %get-tuple-element.39), channel_id=1, source_target_pairs={{1,0},{2,1},{3,2},{4,3},{5,4},{6,5},{7,6},{9,8},{10,9},{11,10},{12... | collective-permute-start | bytes 589832 | tf_op jit(solution)/shard_map/ppermute | solution.py:290
  205.5 11.8 %collective-permute-start.15 = (bf16[3,8,4096]{2,1,0:T(8,128)(2,1)S(1)}, bf16[3,8,4096]{2,1,0:T(8,128)(2,1)S(1)}, u32[]{:S(2)}, u32[]{:S(2)}) collective-permute-start(bf16[3,8,4096]{2,1,0:T(8,128)(2,1)S(1)} %get-tuple-element.38), channel_id=1, source_target_pairs={{1,0},{2,1},{3,2},{4,3},{5,4},{6,5},{7,6},{9,8},{10,9},{11,10},{12... | collective-permute-start | bytes 589832 | tf_op jit(solution)/shard_map/ppermute | solution.py:290
  208.3 10.0 %collective-permute-start.22 = (f32[2,8,40,512]{3,2,1,0:T(8,128)S(1)}, f32[2,8,40,512]{3,2,1,0:T(8,128)S(1)}, u32[]{:S(2)}, u32[]{:S(2)}) collective-permute-start(f32[2,8,40,512]{3,2,1,0:T(8,128)S(1)} %dynamic-slice_bitcast_fusion), channel_id=1, source_target_pairs={{0,8},{8,0},{16,24},{24,16},{1,9},{9,1},{17,25},{25,17},{2,10},{10... | collective-permute-start | bytes 3932168 | tf_op jit(solution)/shard_map/ppermute | solution.py:57
  208.5 11.3 %collective-permute-start.17 = (f32[2,8,40,512]{3,2,1,0:T(8,128)S(1)}, f32[2,8,40,512]{3,2,1,0:T(8,128)S(1)}, u32[]{:S(2)}, u32[]{:S(2)}) collective-permute-start(f32[2,8,40,512]{3,2,1,0:T(8,128)S(1)} %dynamic-slice_bitcast_fusion.1), channel_id=1, source_target_pairs={{0,8},{8,0},{16,24},{24,16},{1,9},{9,1},{17,25},{25,17},{2,10},{10... | collective-permute-start | bytes 3932168 | tf_op jit(solution)/shard_map/ppermute | solution.py:57
  218.6 10.7 %collective-permute-start.23 = (bf16[1,8,40,512]{3,2,1,0:T(8,128)(2,1)S(1)}, bf16[1,8,40,512]{3,2,1,0:T(8,128)(2,1)S(1)}, u32[]{:S(2)}, u32[]{:S(2)}) collective-permute-start(bf16[1,8,40,512]{3,2,1,0:T(8,128)(2,1)S(1)} %dynamic-slice_convert_fusion), channel_id=1, source_target_pairs={{0,16},{8,24},{16,0},{24,8},{1,17},{9,25},{17,1},{25,9},{2,18},{10... | collective-permute-start | bytes 983048 | tf_op jit(solution)/shard_map/ppermute | solution.py:57
  220.1 13.9 %collective-permute-start.18 = (bf16[1,8,40,512]{3,2,1,0:T(8,128)(2,1)S(1)}, bf16[1,8,40,512]{3,2,1,0:T(8,128)(2,1)S(1)}, u32[]{:S(2)}, u32[]{:S(2)}) collective-permute-start(bf16[1,8,40,512]{3,2,1,0:T(8,128)(2,1)S(1)} %dynamic-slice_convert_fusion.1), channel_id=1, source_target_pairs={{0,16},{8,24},{16,0},{24,8},{1,17},{9,25},{17,1},{25,9},{2,18},{10... | collective-permute-start | bytes 983048 | tf_op jit(solution)/shard_map/ppermute | solution.py:57
  229.5 8.9 %collective-permute-start.24 = (bf16[4,40,512]{2,1,0:T(8,128)(2,1)S(1)}, bf16[4,40,512]{2,1,0:T(8,128)(2,1)S(1)}, u32[]{:S(2)}, u32[]{:S(2)}) collective-permute-start(bf16[4,40,512]{2,1,0:T(8,128)(2,1)S(1)} %fusion.2), channel_id=1, source_target_pairs={{0,1},{1,0},{2,3},{3,2},{4,5},{5,4},{6,7},{7,6},{8,9},{9,8},{10,11... | collective-permute-start | bytes 491528 | tf_op jit(solution)/shard_map/ppermute | solution.py:57
  234.2 7.5 %collective-permute-start.19 = (bf16[4,40,512]{2,1,0:T(8,128)(2,1)S(1)}, bf16[4,40,512]{2,1,0:T(8,128)(2,1)S(1)}, u32[]{:S(2)}, u32[]{:S(2)}) collective-permute-start(bf16[4,40,512]{2,1,0:T(8,128)(2,1)S(1)} %fusion.1), channel_id=1, source_target_pairs={{0,1},{1,0},{2,3},{3,2},{4,5},{5,4},{6,7},{7,6},{8,9},{9,8},{10,11... | collective-permute-start | bytes 491528 | tf_op jit(solution)/shard_map/ppermute | solution.py:57
  238.5 5.5 %collective-permute-start.25 = (bf16[2,40,512]{2,1,0:T(8,128)(2,1)S(1)}, bf16[2,40,512]{2,1,0:T(8,128)(2,1)S(1)}, u32[]{:S(2)}, u32[]{:S(2)}) collective-permute-start(bf16[2,40,512]{2,1,0:T(8,128)(2,1)S(1)} %fusion.6), channel_id=1, source_target_pairs={{0,2},{1,3},{2,0},{3,1},{4,6},{5,7},{6,4},{7,5},{8,10},{9,11},{10,... | collective-permute-start | bytes 245768 | tf_op jit(solution)/shard_map/ppermute | solution.py:57
  244.0 5.5 %collective-permute-start.26 = (bf16[1,40,512]{2,1,0:T(8,128)(2,1)S(1)}, bf16[1,40,512]{2,1,0:T(8,128)(2,1)S(1)}, u32[]{:S(2)}, u32[]{:S(2)}) collective-permute-start(bf16[1,40,512]{2,1,0:T(8,128)(2,1)S(1)} %dynamic-slice_convert_fusion.5), channel_id=1, source_target_pairs={{0,4},{1,5},{2,6},{3,7},{4,0},{5,1},{6,2},{7,3},{8,12},{9,13},{10,... | collective-permute-start | bytes 122888 | tf_op jit(solution)/shard_map/ppermute | solution.py:57
  246.4 5.0 %collective-permute-start.21 = (bf16[1,40,512]{2,1,0:T(8,128)(2,1)S(1)}, bf16[1,40,512]{2,1,0:T(8,128)(2,1)S(1)}, u32[]{:S(2)}, u32[]{:S(2)}) collective-permute-start(bf16[1,40,512]{2,1,0:T(8,128)(2,1)S(1)} %dynamic-slice_convert_fusion.6), channel_id=1, source_target_pairs={{0,4},{1,5},{2,6},{3,7},{4,0},{5,1},{6,2},{7,3},{8,12},{9,13},{10,... | collective-permute-start | bytes 122888 | tf_op jit(solution)/shard_map/ppermute | solution.py:57
  (21 other events, 319.3 us)
